TPU v7x, 256 devices: a whole 4x4x8 slice. The times are simulated.
256 devices in a mesh: row: 16 (over y, x), col: 16 (over z, core).
Axes of the slice: x: 4, y: 4, z: 8, core: 2. Of those that a mesh axis runs over, the one named last changes fastest.
Arguments:
- rhs: float32 [2048, 256], P('row'), may hold values from -6 to 6
- sep_lower: bfloat16 [2048, 2048], P('row'), may hold values from -0.5 to 0.5
- sep_pattern: int32 [16, 16], replicated, may hold values 0 or 1
- diag_inverse: bfloat16 [2048, 128], replicated, may hold values from -0.5 to 0.5
- child_lower: bfloat16 [2048, 131072], P('row', 'col'), may hold values from -0.0234375 to 0.0234375
- child_ids: int32 [16, 1024], P('row', 'col'), may hold values from 0 to 31
- child_count: int32 [16, 16], P('row', 'col'), may hold values from 1 to 64, 512 in all within a row
- child_x: bfloat16 [65536, 256], P('col'), may hold values from -6 to 6
Outputs:
- solution: bfloat16 [2048, 256], P('row')
Inputs may be any that keep to these rules, and one draw needn't show every extreme that they name: `child_count`: for each separator block the counts over the 16 process columns sum to 512, and the largest is exactly 64.
All inputs are finite; a program needn't handle non-finite values.
Results may differ from a plain program's by a relative error of at most 0.02.
Values may be sent and summed in bfloat16 or wider, within the bound.
A program may use at most 64 MiB of HBM per device.

v0:
```python
import jax
import jax.numpy as jnp
from jax import lax
from jax.sharding import PartitionSpec as P


def from_root(block, axis, source):
    block = jnp.where(lax.axis_index(axis) == source, block, jnp.zeros_like(block))
    return lax.psum(block, axis)


def child_partial(child_lower, child_ids, child_count, child_x, block_size):
    rhs_width = child_x.shape[1]
    blocks_x = child_x.reshape(-1, block_size, rhs_width)
    slot_total = child_ids.shape[1]
    slot_range = jnp.arange(slot_total, dtype=jnp.int32)

    def one_block(inputs):
        lower_row, ids_row, count_one = inputs
        picked = blocks_x[ids_row]
        live_slots = slot_range < count_one[0]
        picked = jnp.where(live_slots[:, None, None], picked, jnp.zeros((), jnp.bfloat16))
        return jnp.dot(
            lower_row,
            picked.reshape(slot_total * block_size, rhs_width),
            preferred_element_type=jnp.float32,
        )

    lower_rows = child_lower.reshape(child_ids.shape[0], block_size, -1)
    return lax.map(one_block, (lower_rows, child_ids, child_count))


def on_device(
    rhs, sep_lower, sep_pattern, diag_inverse, child_lower, child_ids, child_count, child_x
):
    block_size = diag_inverse.shape[1]
    rhs_width = rhs.shape[1]
    total_blocks = sep_pattern.shape[0]
    my_row = lax.axis_index("row")
    pending = child_partial(child_lower, child_ids, child_count, child_x, block_size)[0]

    def local_term(position, solved):
        column = lax.dynamic_slice_in_dim(sep_lower, position * block_size, block_size, 1)
        flag = sep_pattern[my_row, position]
        keep_mask = (flag > 0) & (my_row > position)
        new_terms = jnp.dot(column, solved, preferred_element_type=jnp.float32)
        return new_terms * keep_mask.astype(jnp.float32)

    def solve_local(position, own_rhs, summed):
        residual = (own_rhs - summed).astype(jnp.bfloat16)
        inverse = lax.dynamic_slice_in_dim(diag_inverse, position * block_size, block_size, 0)
        return jnp.dot(inverse, residual, preferred_element_type=jnp.float32).astype(jnp.bfloat16)

    summed = lax.psum(pending, "col")
    result = jnp.zeros((block_size, rhs_width), jnp.bfloat16)

    def advance(position, state_now):
        running, kept = state_now
        solved = from_root(solve_local(position, rhs, running), "row", position)
        running = running + local_term(position, solved)
        kept = jnp.where(my_row == position, solved, kept)
        return (running, kept)

    summed, result = lax.fori_loop(0, total_blocks, advance, (summed, result))
    return result


def solution(mesh):
    in_specs = (
        P("row", None),
        P("row", None),
        P(),
        P(),
        P("row", "col"),
        P("row", "col"),
        P("row", "col"),
        P("col", None),
    )
    out_specs = P("row", None)
    return jax.shard_map(
        on_device, mesh=mesh, in_specs=in_specs, out_specs=out_specs, check_vma=False
    )
```

profile of v0, /device:TPU:24, one launch (start us, length us, event | category | flops | bytes accessed | tf_op | source)
XLA Modules:
  0.0 1672.4 jit_solution(3951890338432846664)
XLA Ops:
  8.1 2.7 gather_fusion
  10.9 6.1 bitcast_select_fusion
  17.0 1.9 convolution_bitcast_fusion
  19.0 110.2 %all-reduce.3.cloned.1.call-done = f32[128,256]{0,1:T(8,128)} async-done(((f32[128,256]{0,1:T(8,128)}), f32[128,256]{0,1:T(8,128)}) %all-reduce.3.cloned.1.call-update) | async-done | bytes 131088 | tf_op jit(solution)/shard_map/psum | solution.py:54
  130.2 1535.1 %while.22 = (s32[]{:T(128)}, f32[128,256]{1,0:T(8,128)S(1)}, bf16[128,256]{1,0:T(8,128)(2,1)S(1)}, bf16[128,2048]{1,0:T(8,128)(2,1)}, bf16[2048,128]{1,0:T(8,128...) while((s32[]{:T(128)}, f32[128,256]{1,0:T(8,128)S(1)}, ...), condition=%wide.region_3.4_spmd.clone, body=%wide.region_1.3_spmd.clone.sunk | while | flops 17072140 | bytes 1311075 | solution.py:64
  133.8 91.9 %all-reduce.5.cloned.1.call-done = bf16[128,256]{1,0:T(8,128)(2,1)} async-done(((bf16[128,256]{1,0:T(8,128)(2,1)}), bf16[128,256]{1,0:T(8,128)(2,1)}) %all-reduce.5.cloned.1.call-update) | async-done | bytes 65552 | tf_op jit(solution)/shard_map/while/body/eval_jaxpr/psum | solution.py:9
  226.8 1.5 fusion.18
  230.4 91.3 %all-reduce.5.cloned.1.call-done = bf16[128,256]{1,0:T(8,128)(2,1)} async-done(((bf16[128,256]{1,0:T(8,128)(2,1)}), bf16[128,256]{1,0:T(8,128)(2,1)}) %all-reduce.5.cloned.1.call-update) | async-done | bytes 65552 | tf_op jit(solution)/shard_map/while/body/eval_jaxpr/psum | solution.py:9
  322.8 1.5 fusion.18
  326.3 90.9 %all-reduce.5.cloned.1.call-done = bf16[128,256]{1,0:T(8,128)(2,1)} async-done(((bf16[128,256]{1,0:T(8,128)(2,1)}), bf16[128,256]{1,0:T(8,128)(2,1)}) %all-reduce.5.cloned.1.call-update) | async-done | bytes 65552 | tf_op jit(solution)/shard_map/while/body/eval_jaxpr/psum | solution.py:9
  418.4 1.5 fusion.18
  422.0 91.0 %all-reduce.5.cloned.1.call-done = bf16[128,256]{1,0:T(8,128)(2,1)} async-done(((bf16[128,256]{1,0:T(8,128)(2,1)}), bf16[128,256]{1,0:T(8,128)(2,1)}) %all-reduce.5.cloned.1.call-update) | async-done | bytes 65552 | tf_op jit(solution)/shard_map/while/body/eval_jaxpr/psum | solution.py:9
  514.1 1.5 fusion.18
  517.6 90.9 %all-reduce.5.cloned.1.call-done = bf16[128,256]{1,0:T(8,128)(2,1)} async-done(((bf16[128,256]{1,0:T(8,128)(2,1)}), bf16[128,256]{1,0:T(8,128)(2,1)}) %all-reduce.5.cloned.1.call-update) | async-done | bytes 65552 | tf_op jit(solution)/shard_map/while/body/eval_jaxpr/psum | solution.py:9
  609.7 1.5 fusion.18
  613.3 91.3 %all-reduce.5.cloned.1.call-done = bf16[128,256]{1,0:T(8,128)(2,1)} async-done(((bf16[128,256]{1,0:T(8,128)(2,1)}), bf16[128,256]{1,0:T(8,128)(2,1)}) %all-reduce.5.cloned.1.call-update) | async-done | bytes 65552 | tf_op jit(solution)/shard_map/while/body/eval_jaxpr/psum | solution.py:9
  705.7 1.5 fusion.18
  709.3 91.3 %all-reduce.5.cloned.1.call-done = bf16[128,256]{1,0:T(8,128)(2,1)} async-done(((bf16[128,256]{1,0:T(8,128)(2,1)}), bf16[128,256]{1,0:T(8,128)(2,1)}) %all-reduce.5.cloned.1.call-update) | async-done | bytes 65552 | tf_op jit(solution)/shard_map/while/body/eval_jaxpr/psum | solution.py:9
  801.7 1.5 fusion.18
  805.2 91.2 %all-reduce.5.cloned.1.call-done = bf16[128,256]{1,0:T(8,128)(2,1)} async-done(((bf16[128,256]{1,0:T(8,128)(2,1)}), bf16[128,256]{1,0:T(8,128)(2,1)}) %all-reduce.5.cloned.1.call-update) | async-done | bytes 65552 | tf_op jit(solution)/shard_map/while/body/eval_jaxpr/psum | solution.py:9
  897.6 1.5 fusion.18
  901.2 91.0 %all-reduce.5.cloned.1.call-done = bf16[128,256]{1,0:T(8,128)(2,1)} async-done(((bf16[128,256]{1,0:T(8,128)(2,1)}), bf16[128,256]{1,0:T(8,128)(2,1)}) %all-reduce.5.cloned.1.call-update) | async-done | bytes 65552 | tf_op jit(solution)/shard_map/while/body/eval_jaxpr/psum | solution.py:9
  993.3 1.5 fusion.18
  996.8 91.2 %all-reduce.5.cloned.1.call-done = bf16[128,256]{1,0:T(8,128)(2,1)} async-done(((bf16[128,256]{1,0:T(8,128)(2,1)}), bf16[128,256]{1,0:T(8,128)(2,1)}) %all-reduce.5.cloned.1.call-update) | async-done | bytes 65552 | tf_op jit(solution)/shard_map/while/body/eval_jaxpr/psum | solution.py:9
  1092.8 90.9 %all-reduce.5.cloned.1.call-done = bf16[128,256]{1,0:T(8,128)(2,1)} async-done(((bf16[128,256]{1,0:T(8,128)(2,1)}), bf16[128,256]{1,0:T(8,128)(2,1)}) %all-reduce.5.cloned.1.call-update) | async-done | bytes 65552 | tf_op jit(solution)/shard_map/while/body/eval_jaxpr/psum | solution.py:9
  1188.4 92.1 %all-reduce.5.cloned.1.call-done = bf16[128,256]{1,0:T(8,128)(2,1)} async-done(((bf16[128,256]{1,0:T(8,128)(2,1)}), bf16[128,256]{1,0:T(8,128)(2,1)}) %all-reduce.5.cloned.1.call-update) | async-done | bytes 65552 | tf_op jit(solution)/shard_map/while/body/eval_jaxpr/psum | solution.py:9
  1285.2 91.5 %all-reduce.5.cloned.1.call-done = bf16[128,256]{1,0:T(8,128)(2,1)} async-done(((bf16[128,256]{1,0:T(8,128)(2,1)}), bf16[128,256]{1,0:T(8,128)(2,1)}) %all-reduce.5.cloned.1.call-update) | async-done | bytes 65552 | tf_op jit(solution)/shard_map/while/body/eval_jaxpr/psum | solution.py:9
  1378.7 1.6 fusion.18
  1382.3 90.1 %all-reduce.5.cloned.1.call-done = bf16[128,256]{1,0:T(8,128)(2,1)} async-done(((bf16[128,256]{1,0:T(8,128)(2,1)}), bf16[128,256]{1,0:T(8,128)(2,1)}) %all-reduce.5.cloned.1.call-update) | async-done | bytes 65552 | tf_op jit(solution)/shard_map/while/body/eval_jaxpr/psum | solution.py:9
  1477.1 90.9 %all-reduce.5.cloned.1.call-done = bf16[128,256]{1,0:T(8,128)(2,1)} async-done(((bf16[128,256]{1,0:T(8,128)(2,1)}), bf16[128,256]{1,0:T(8,128)(2,1)}) %all-reduce.5.cloned.1.call-update) | async-done | bytes 65552 | tf_op jit(solution)/shard_map/while/body/eval_jaxpr/psum | solution.py:9
  1569.2 1.5 fusion.18
  1572.7 91.5 %all-reduce.5.cloned.1.call-done = bf16[128,256]{1,0:T(8,128)(2,1)} async-done(((bf16[128,256]{1,0:T(8,128)(2,1)}), bf16[128,256]{1,0:T(8,128)(2,1)}) %all-reduce.5.cloned.1.call-update) | async-done | bytes 65552 | tf_op jit(solution)/shard_map/while/body/eval_jaxpr/psum | solution.py:9
  (101 shorter events, 50.1 us)
Async XLA Ops:
  6.5 1.6 copy-start
  6.5 122.6 %all-reduce.3.cloned.1.call-start = ((), (), s32[]{:S(2)}) async-start(), calls=%async_computation | async-start | bytes 262144 | tf_op jit(solution)/shard_map/psum | solution.py:54
  10.9 6.1 copy-start.2
  17.0 113.2 %copy-start.1 = (f32[128,256]{1,0:T(8,128)S(1)}, f32[128,256]{1,0:T(8,128)}, u32[]{:S(2)}) copy-start(f32[128,256]{1,0:T(8,128)} %param.10) | copy-start | bytes 393220
  130.2 95.5 %all-reduce.5.cloned.1.call-start = ((), (), s32[]{:S(2)}) async-start(), calls=%async_computation.1 | async-start | bytes 131072 | tf_op jit(solution)/shard_map/while/body/eval_jaxpr/psum | solution.py:9
  226.8 94.9 %all-reduce.5.cloned.1.call-start = ((), (), s32[]{:S(2)}) async-start(), calls=%async_computation.1 | async-start | bytes 131072 | tf_op jit(solution)/shard_map/while/body/eval_jaxpr/psum | solution.py:9
  322.7 94.6 %all-reduce.5.cloned.1.call-start = ((), (), s32[]{:S(2)}) async-start(), calls=%async_computation.1 | async-start | bytes 131072 | tf_op jit(solution)/shard_map/while/body/eval_jaxpr/psum | solution.py:9
  418.4 94.6 %all-reduce.5.cloned.1.call-start = ((), (), s32[]{:S(2)}) async-start(), calls=%async_computation.1 | async-start | bytes 131072 | tf_op jit(solution)/shard_map/while/body/eval_jaxpr/psum | solution.py:9
  514.0 94.6 %all-reduce.5.cloned.1.call-start = ((), (), s32[]{:S(2)}) async-start(), calls=%async_computation.1 | async-start | bytes 131072 | tf_op jit(solution)/shard_map/while/body/eval_jaxpr/psum | solution.py:9
  609.7 94.9 %all-reduce.5.cloned.1.call-start = ((), (), s32[]{:S(2)}) async-start(), calls=%async_computation.1 | async-start | bytes 131072 | tf_op jit(solution)/shard_map/while/body/eval_jaxpr/psum | solution.py:9
  705.6 94.9 %all-reduce.5.cloned.1.call-start = ((), (), s32[]{:S(2)}) async-start(), calls=%async_computation.1 | async-start | bytes 131072 | tf_op jit(solution)/shard_map/while/body/eval_jaxpr/psum | solution.py:9
  801.6 94.9 %all-reduce.5.cloned.1.call-start = ((), (), s32[]{:S(2)}) async-start(), calls=%async_computation.1 | async-start | bytes 131072 | tf_op jit(solution)/shard_map/while/body/eval_jaxpr/psum | solution.py:9
  897.5 94.6 %all-reduce.5.cloned.1.call-start = ((), (), s32[]{:S(2)}) async-start(), calls=%async_computation.1 | async-start | bytes 131072 | tf_op jit(solution)/shard_map/while/body/eval_jaxpr/psum | solution.py:9
  993.2 94.9 %all-reduce.5.cloned.1.call-start = ((), (), s32[]{:S(2)}) async-start(), calls=%async_computation.1 | async-start | bytes 131072 | tf_op jit(solution)/shard_map/while/body/eval_jaxpr/psum | solution.py:9
  1089.1 94.6 %all-reduce.5.cloned.1.call-start = ((), (), s32[]{:S(2)}) async-start(), calls=%async_computation.1 | async-start | bytes 131072 | tf_op jit(solution)/shard_map/while/body/eval_jaxpr/psum | solution.py:9
  1184.8 95.7 %all-reduce.5.cloned.1.call-start = ((), (), s32[]{:S(2)}) async-start(), calls=%async_computation.1 | async-start | bytes 131072 | tf_op jit(solution)/shard_map/while/body/eval_jaxpr/psum | solution.py:9
  1281.6 95.1 %all-reduce.5.cloned.1.call-start = ((), (), s32[]{:S(2)}) async-start(), calls=%async_computation.1 | async-start | bytes 131072 | tf_op jit(solution)/shard_map/while/body/eval_jaxpr/psum | solution.py:9
  1378.6 93.7 %all-reduce.5.cloned.1.call-start = ((), (), s32[]{:S(2)}) async-start(), calls=%async_computation.1 | async-start | bytes 131072 | tf_op jit(solution)/shard_map/while/body/eval_jaxpr/psum | solution.py:9
  1473.4 94.6 %all-reduce.5.cloned.1.call-start = ((), (), s32[]{:S(2)}) async-start(), calls=%async_computation.1 | async-start | bytes 131072 | tf_op jit(solution)/shard_map/while/body/eval_jaxpr/psum | solution.py:9
  1569.1 95.1 %all-reduce.5.cloned.1.call-start = ((), (), s32[]{:S(2)}) async-start(), calls=%async_computation.1 | async-start | bytes 131072 | tf_op jit(solution)/shard_map/while/body/eval_jaxpr/psum | solution.py:9
  1665.3 0.6 copy-start.3
Sparse Core Ops, SparseCore 0:
  19.1 110.0 all-reduce.2
  134.6 91.0 all-reduce.4
  231.1 90.4 all-reduce.4
  326.8 90.4 all-reduce.4
  422.4 90.4 all-reduce.4
  518.1 90.4 all-reduce.4
  614.0 90.4 all-reduce.4
  710.0 90.4 all-reduce.4
  805.9 90.4 all-reduce.4
  901.6 90.4 all-reduce.4
  997.6 90.4 all-reduce.4
  1093.2 90.4 all-reduce.4
  1189.2 91.3 all-reduce.4
  1285.6 91.0 all-reduce.4
  1382.7 89.6 all-reduce.4
  1477.5 90.4 all-reduce.4
  1573.1 90.9 all-reduce.4
where the time goes:
time: 1680 us; the launch traced here: 1670 us
  waiting for transfers between devices  1570 us (93%)
  matrix products  42.9 us (3%)
  local copies, waits for them, and re-layouts  25.7 us (2%)
    psum x16, waiting for transfers between devices, from_root(): return lax.psum(block, axis)  1460 us
    psum x1, waiting for transfers between devices, on_device(): summed = lax.psum(pending, 'col')  110 us
  transfers between devices with their start and end apart: 17, of which 17 were waited for; matrix products, arithmetic and copies ran while one was open for 1% of the time, Pallas kernels for 0%

commit v1 on v0

v1 whole, which is shorter than its diff:
```python
import jax
import jax.numpy as jnp
from jax import lax
from jax.experimental import pallas as pl
from jax.experimental.pallas import tpu as pltpu
from jax.sharding import PartitionSpec as P

MESH = pl.DeviceIdType.MESH
BF16 = jnp.bfloat16
F32 = jnp.float32

ROWS = 16
COLS = 16
CHIPS = COLS // 2
BS = 128
WIDTH = 256
PART = WIDTH // CHIPS
LAST = ROWS - 1
SLOTS = 64
BLOCKS = 32
CHUNKS = 4
VIA = {10: 14}
FAR_FIRST = (4, 3, 5, 2, 6, 1, 7)


def dot_t(a, b):
    return lax.dot_general(a, b, (((1,), (1,)), ((), ())), preferred_element_type=F32)


def kernel(
    pattern, ids, count, rhs_hbm, sep_hbm, dinv_hbm, lower_hbm, x_hbm, out,
    x_all, lower, sep, dinv, rhs, scaled, factor, relay, sums, parts, rhs_t,
    residual, residuals, solved, result,
    load_sem, factor_send, factor_recv, relay_sem, part_send, part_recv,
    residual_send, residual_recv, solved_send, result_send, result_recv,
):
    row, col = lax.axis_index("row"), lax.axis_index("col")
    chip, core = col // 2, lax.rem(col, 2)
    first = core == 0
    solver = first & (row == LAST)

    def other_chip(step):
        return lax.rem(chip + step, CHIPS)

    barrier = pltpu.get_barrier_semaphore()

    def greet(r, c):
        pl.semaphore_signal(barrier, inc=1, device_id=(r, c), device_id_type=MESH)

    for step in FAR_FIRST:
        greet(row, 2 * other_chip(step))

        @pl.when(first)
        def _():
            greet(row, 2 * other_chip(step) + 1)

    greet(row, 2 * chip + 1 - core)

    @pl.when(first & (row != LAST))
    def _():
        greet(LAST, col)

    @pl.when(solver)
    def _():
        for r in range(LAST):
            greet(r, col)

    for a, b in VIA.items():
        @pl.when(first & (row == a))
        def _():
            greet(b, col)

        @pl.when(first & (row == b))
        def _():
            greet(a, col)

    def load(src, dst, sem):
        copy = pltpu.make_async_copy(src, dst, load_sem.at[sem])
        copy.start()
        return copy

    load_sep = load(sep_hbm, sep, 0)
    load_dinv = load(dinv_hbm, dinv, 1)
    load_x = load(x_hbm, x_all.at[pl.ds(0, BLOCKS)], 2)
    span = SLOTS * BS // CHUNKS
    load_lower = [
        load(lower_hbm.at[:, pl.ds(i * span, span)], lower.at[i], 4 + i) for i in range(CHUNKS)
    ]
    load_rhs = load(rhs_hbm, rhs, 3)
    x_all[BLOCKS] = jnp.zeros((BS, WIDTH), BF16)

    load_sep.wait()
    load_dinv.wait()

    @pl.when(first)
    def _():
        own = dinv[pl.ds(pl.multiple_of(row * BS, BS), BS), :]
        for j in range(LAST):
            term = jnp.dot(own, sep[:, j * BS:(j + 1) * BS], preferred_element_type=F32)
            scaled[j] = (term * pattern[row, j].astype(F32)).astype(BF16)

    load_x.wait()
    live = count[0, 0]
    total = jnp.zeros((BS, WIDTH), F32)
    pairs = SLOTS // 2 // CHUNKS
    for i in range(CHUNKS):
        load_lower[i].wait()
        for p in range(pairs):
            j = 2 * (i * pairs + p)
            picked = [x_all[jnp.where(s < live, ids[0, s], BLOCKS)] for s in (j, j + 1)]
            total += jnp.dot(
                lower[i, :, 2 * p * BS:2 * (p + 1) * BS],
                jnp.concatenate(picked, 0),
                preferred_element_type=F32,
            )
    sums[...] = total.T.reshape(CHIPS, PART, BS)
    load_rhs.wait()
    rhs_t[...] = rhs[...].T.reshape(CHIPS, PART, BS)

    via_count = jnp.where((row == 10) | (row == 14), 1, 0)
    pl.semaphore_wait(
        barrier,
        jnp.where(first, COLS - 1 + jnp.where(row == LAST, LAST, 1) + via_count, CHIPS),
    )

    def factor_copy(r):
        via = VIA.get(r)
        if via is None:
            return pltpu.make_async_remote_copy(
                src_ref=scaled.at[pl.ds(0, r)], dst_ref=factor.at[r, pl.ds(0, r)],
                send_sem=factor_send.at[0], recv_sem=factor_recv.at[r],
                device_id=(LAST, col), device_id_type=MESH)
        return pltpu.make_async_remote_copy(
            src_ref=scaled.at[pl.ds(0, r)], dst_ref=relay.at[pl.ds(0, r)],
            send_sem=factor_send.at[0], recv_sem=relay_sem.at[0],
            device_id=(via, col), device_id_type=MESH)

    def relay_copy(r):
        return pltpu.make_async_remote_copy(
            src_ref=relay.at[pl.ds(0, r)], dst_ref=factor.at[r, pl.ds(0, r)],
            send_sem=relay_sem.at[1], recv_sem=factor_recv.at[r],
            device_id=(LAST, col), device_id_type=MESH)

    for r in range(1, LAST):
        @pl.when(first & (row == r))
        def _():
            factor_copy(r).start()

    def part_copy(step):
        to = other_chip(step)
        return pltpu.make_async_remote_copy(
            src_ref=sums.at[to], dst_ref=parts.at[col],
            send_sem=part_send.at[step], recv_sem=part_recv.at[col],
            device_id=(row, 2 * to), device_id_type=MESH)

    for step in FAR_FIRST:
        part_copy(step).start()

    @pl.when(jnp.logical_not(first))
    def _():
        part_copy(0).start()

    def residual_copy():
        return pltpu.make_async_remote_copy(
            src_ref=residual, dst_ref=residuals.at[row],
            send_sem=residual_send.at[0], recv_sem=residual_recv.at[row],
            device_id=(LAST, col), device_id_type=MESH)

    def result_copy(step, to_core):
        return pltpu.make_async_remote_copy(
            src_ref=result.at[chip], dst_ref=result.at[chip],
            send_sem=result_send.at[step, to_core], recv_sem=result_recv.at[chip],
            device_id=(row, 2 * other_chip(step) + to_core), device_id_type=MESH)

    def solved_copy(r):
        return pltpu.make_async_remote_copy(
            src_ref=solved.at[r], dst_ref=result.at[chip],
            send_sem=solved_send.at[r], recv_sem=result_recv.at[chip],
            device_id=(r, col), device_id_type=MESH)

    def result_wait(at):
        pltpu.make_async_remote_copy(
            src_ref=solved.at[0], dst_ref=result.at[at],
            send_sem=result_send.at[0, 0], recv_sem=result_recv.at[at],
            device_id=(row, col), device_id_type=MESH).wait_recv()

    @pl.when(first)
    def _():
        parts[col] = sums[chip]
        for k in range(1, COLS):
            src = lax.rem(col + k, COLS)
            pltpu.make_async_remote_copy(
                src_ref=sums.at[0], dst_ref=parts.at[src],
                send_sem=part_send.at[0], recv_sem=part_recv.at[src],
                device_id=(row, col), device_id_type=MESH).wait_recv()
        summed = parts[0]
        for k in range(1, COLS):
            summed += parts[k]
        value = (rhs_t[chip] - summed).astype(BF16)

        @pl.when(row != LAST)
        def _():
            residual[...] = value
            residual_copy().start()

        @pl.when(row == LAST)
        def _():
            residuals[LAST] = value

    for r, via in VIA.items():
        @pl.when(first & (row == via))
        def _():
            pltpu.make_async_remote_copy(
                src_ref=scaled.at[pl.ds(0, r)], dst_ref=relay.at[pl.ds(0, r)],
                send_sem=factor_send.at[0], recv_sem=relay_sem.at[0],
                device_id=(LAST, col), device_id_type=MESH).wait_recv()
            relay_copy(r).start()

    @pl.when(solver)
    def _():
        done = []
        for r in range(ROWS):
            if r < LAST:
                pltpu.make_async_remote_copy(
                    src_ref=residual, dst_ref=residuals.at[r],
                    send_sem=residual_send.at[0], recv_sem=residual_recv.at[r],
                    device_id=(LAST, col), device_id_type=MESH).wait_recv()
            if 0 < r < LAST:
                pltpu.make_async_remote_copy(
                    src_ref=scaled.at[pl.ds(0, r)], dst_ref=factor.at[r, pl.ds(0, r)],
                    send_sem=factor_send.at[0], recv_sem=factor_recv.at[r],
                    device_id=(LAST, col), device_id_type=MESH).wait_recv()
            block = dot_t(residuals[r], dinv[r * BS:(r + 1) * BS, :])
            if r:
                blocks = [factor[r, j] if r < LAST else scaled[j] for j in range(r)]
                block -= dot_t(jnp.concatenate(done, 1), jnp.concatenate(blocks, 1))
            block = block.astype(BF16)
            done.append(block)
            if r < LAST:
                solved[r] = block
                solved_copy(r).start()
            else:
                result[chip] = block

    @pl.when(first)
    def _():
        @pl.when(row != LAST)
        def _():
            result_wait(chip)

        for step in FAR_FIRST:
            for to_core in range(2):
                result_copy(step, to_core).start()
        result_copy(0, 1).start()

    for step in range(1, CHIPS):
        result_wait(other_chip(step))

    @pl.when(jnp.logical_not(first))
    def _():
        result_wait(chip)

    out[...] = result[...].reshape(WIDTH, BS)

    for r in range(1, LAST):
        @pl.when(first & (row == r))
        def _():
            factor_copy(r).wait_send()
    for r, via in VIA.items():
        @pl.when(first & (row == via))
        def _():
            relay_copy(r).wait_send()
    for step in FAR_FIRST:
        part_copy(step).wait_send()

    @pl.when(jnp.logical_not(first))
    def _():
        part_copy(0).wait_send()

    @pl.when(first)
    def _():
        @pl.when(row != LAST)
        def _():
            residual_copy().wait_send()

        for step in FAR_FIRST:
            for to_core in range(2):
                result_copy(step, to_core).wait_send()
        result_copy(0, 1).wait_send()

    @pl.when(solver)
    def _():
        for r in range(LAST):
            solved_copy(r).wait_send()


def on_device(
    rhs, sep_lower, sep_pattern, diag_inverse, child_lower, child_ids, child_count, child_x
):
    smem = pl.BlockSpec(memory_space=pltpu.SMEM)
    hbm = pl.BlockSpec(memory_space=pl.ANY)
    dma = pltpu.SemaphoreType.DMA
    found = pl.pallas_call(
        kernel,
        out_shape=jax.ShapeDtypeStruct((WIDTH, BS), BF16),
        in_specs=[smem] * 3 + [hbm] * 5,
        out_specs=pl.BlockSpec(memory_space=pltpu.VMEM),
        scratch_shapes=[
            pltpu.VMEM((BLOCKS + 1, BS, WIDTH), BF16),
            pltpu.VMEM((CHUNKS, BS, SLOTS * BS // CHUNKS), BF16),
            pltpu.VMEM((BS, ROWS * BS), BF16),
            pltpu.VMEM((ROWS * BS, BS), BF16),
            pltpu.VMEM((BS, WIDTH), F32),
            pltpu.VMEM((LAST, BS, BS), BF16),
            pltpu.VMEM((LAST, LAST - 1, BS, BS), BF16),
            pltpu.VMEM((10, BS, BS), BF16),
            pltpu.VMEM((CHIPS, PART, BS), F32),
            pltpu.VMEM((COLS, PART, BS), F32),
            pltpu.VMEM((CHIPS, PART, BS), F32),
            pltpu.VMEM((PART, BS), BF16),
            pltpu.VMEM((ROWS, PART, BS), BF16),
            pltpu.VMEM((LAST, PART, BS), BF16),
            pltpu.VMEM((CHIPS, PART, BS), BF16),
            dma((4 + CHUNKS,)),
            dma((1,)),
            dma((ROWS,)),
            dma((2,)),
            dma((CHIPS,)),
            dma((COLS,)),
            dma((1,)),
            dma((ROWS,)),
            dma((ROWS,)),
            dma((CHIPS, 2)),
            dma((CHIPS,)),
        ],
        compiler_params=pltpu.CompilerParams(
            collective_id=0, has_side_effects=True, vmem_limit_bytes=48 * 2**20
        ),
    )(
        sep_pattern, child_ids, child_count, rhs, sep_lower, diag_inverse, child_lower,
        child_x.reshape(BLOCKS, BS, WIDTH),
    )
    return found.T


def solution(mesh):
    in_specs = (
        P("row", None),
        P("row", None),
        P(),
        P(),
        P("row", "col"),
        P("row", "col"),
        P("row", "col"),
        P("col", None),
    )
    return jax.shard_map(
        on_device, mesh=mesh, in_specs=in_specs, out_specs=P("row", None), check_vma=False
    )
```

time: 1680 us -> 42.5 us (0.03)
  waiting for transfers between devices: 1570 us -> 0 us
  matrix products: 42.9 us -> 0 us
  Pallas kernels: 0 us -> 33.1 us
  local copies, waits for them, and re-layouts: 25.7 us -> 8.25 us
    psum x17 -> x0, waiting for transfers between devices: 1570 us -> none  [the longest x16 1460 us: from_root(): return lax.psum(block, axis)]
    dot_general x33 -> x0, matrix products: 42.9 us -> none  [the longest x16 24.8 us: solve_local(): jnp.dot(inverse, residual, preferred_element_type=jnp.float32)]
    pallas_call x0 -> x1, Pallas kernels: none -> 33.1 us  [on_device(): pl.pallas_call(kernel, out_shape=jax.ShapeDtypeStruct((WIDTH, BS), BF16),...]
    dynamic_slice x16 -> x0, local copies, waits for them, and re-layouts: 21.2 us -> none  [local_term(): flag = sep_pattern[my_row, position]]
  transfers between devices with their start and end apart: 17 -> 0, of which waited for: 17 -> 0; matrix products, arithmetic and copies ran while one was open for 1% -> 0% of each run, Pallas kernels for 0% -> 0%
where the time goes in v1:
time: 42.5 us; the launch traced here: 42 us
  Pallas kernels  33.1 us (78%)
  local copies, waits for them, and re-layouts  8.25 us (19%)
  between operations  0.67 us (2%)
    pallas_call x1, Pallas kernels, on_device(): pl.pallas_call(kernel, out_shape=jax.ShapeDtypeStruct((WIDTH, BS), BF16),...  33.1 us
    unnamed x14, local copies, waits for them, and re-layouts  7.51 us

profile of v1, /device:TPU:24, one launch (start us, length us, event | category | flops | bytes accessed | tf_op | source)
XLA Modules:
  0.0 42.0 jit_solution(6110717452811979796)
XLA Ops:
  0.7 0.0 copy-start
  0.7 1.6 %copy-done = bf16[128,8192]{1,0:T(8,128)(2,1)S(1)} copy-done((bf16[128,8192]{1,0:T(8,128)(2,1)S(1)}, bf16[128,8192]{1,0:T(8,128)(2,1)}, u32[]{:S(2)}) %copy-start) | copy-done | bytes 2097176
  2.2 0.0 copy-start.1
  2.2 1.6 %copy-done.1 = bf16[4096,256]{1,0:T(8,128)(2,1)S(1)} copy-done((bf16[4096,256]{1,0:T(8,128)(2,1)S(1)}, bf16[4096,256]{1,0:T(8,128)(2,1)}, u32[]{:S(2)}) %copy-start.1) | copy-done | bytes 2097176
  3.8 0.0 copy-start.2
  3.8 1.0 %copy-done.2 = bf16[128,2048]{1,0:T(8,128)(2,1)S(1)} copy-done((bf16[128,2048]{1,0:T(8,128)(2,1)S(1)}, bf16[128,2048]{1,0:T(8,128)(2,1)}, u32[]{:S(2)}) %copy-start.2) | copy-done | bytes 524312
  4.9 0.0 copy-start.3
  4.9 1.0 %copy-done.3 = bf16[2048,128]{1,0:T(8,128)(2,1)S(1)} copy-done((bf16[2048,128]{1,0:T(8,128)(2,1)S(1)}, bf16[2048,128]{1,0:T(8,128)(2,1)}, u32[]{:S(2)}) %copy-start.3) | copy-done | bytes 524312
  5.9 0.0 copy-start.4
  5.9 0.9 %copy-done.4 = f32[128,256]{1,0:T(8,128)S(1)} copy-done((f32[128,256]{1,0:T(8,128)S(1)}, f32[128,256]{1,0:T(8,128)}, u32[]{:S(2)}) %copy-start.4) | copy-done | bytes 131096
  6.8 0.0 copy-start.5
  6.8 0.7 %copy-done.5 = s32[16,16]{1,0:T(8,128)S(1)} copy-done((s32[16,16]{1,0:T(8,128)S(1)}, s32[16,16]{1,0:T(8,128)}, u32[]{:S(2)}) %copy-start.5) | copy-done | bytes 1048
  7.5 0.0 copy-start.6
  7.5 0.7 %copy-done.6 = s32[1,64]{1,0:T(1,128)S(1)} copy-done((s32[1,64]{1,0:T(1,128)S(1)}, s32[1,64]{1,0:T(1,128)}, u32[]{:S(2)}) %copy-start.6) | copy-done | bytes 280
  8.2 33.1 %shard_map.82 = bf16[256,128]{1,0:T(8,128)(2,1)S(1)} custom-call(s32[16,16]{1,0:T(8,128)S(1)} %copy-done.5, s32[1,64]{1,0:T(1,128)S(1)} %copy-done.6, s32[1,1]{1,0:T(1,128)S(6)} %copy.10.count, f32[128,256]{1,0:T(8,128)S(1)} %copy-done.4, bf16[128,2048]{1,0:T(8,128)(2,1)S(1)} %copy-done.2, bf16[2048,128]{1,0:T(8,128)(2,1)S(1)} %copy-done.3, ...), custom_call_target="tpu_custom_call" | custom-call | tf_op jit(solution)/shard_map/pallas_call | solution.py:303
  41.3 0.7 %copy.9 = bf16[128,256]{1,0:T(8,128)(2,1)} copy(bf16[128,256]{0,1:T(8,128)(2,1)S(1)} %bitcast.3) | data formatting | bytes 131072 | tf_op jit(solution)/shard_map/transpose | solution.py:343
Async XLA Ops:
  0.7 1.6 %copy-start = (bf16[128,8192]{1,0:T(8,128)(2,1)S(1)}, bf16[128,8192]{1,0:T(8,128)(2,1)}, u32[]{:S(2)}) copy-start(bf16[128,8192]{1,0:T(8,128)(2,1)} %lower_hbm.1) | copy-start | bytes 6291460
  2.2 1.6 %copy-start.1 = (bf16[4096,256]{1,0:T(8,128)(2,1)S(1)}, bf16[4096,256]{1,0:T(8,128)(2,1)}, u32[]{:S(2)}) copy-start(bf16[4096,256]{1,0:T(8,128)(2,1)} %param.15) | copy-start | bytes 6291460
  3.8 1.0 %copy-start.2 = (bf16[128,2048]{1,0:T(8,128)(2,1)S(1)}, bf16[128,2048]{1,0:T(8,128)(2,1)}, u32[]{:S(2)}) copy-start(bf16[128,2048]{1,0:T(8,128)(2,1)} %sep_hbm.1) | copy-start | bytes 1572868
  4.9 1.0 %copy-start.3 = (bf16[2048,128]{1,0:T(8,128)(2,1)S(1)}, bf16[2048,128]{1,0:T(8,128)(2,1)}, u32[]{:S(2)}) copy-start(bf16[2048,128]{1,0:T(8,128)(2,1)} %dinv_hbm.1) | copy-start | bytes 1572868
  5.9 0.9 %copy-start.4 = (f32[128,256]{1,0:T(8,128)S(1)}, f32[128,256]{1,0:T(8,128)}, u32[]{:S(2)}) copy-start(f32[128,256]{1,0:T(8,128)} %rhs_hbm.1) | copy-start | bytes 393220
  6.8 0.7 %copy-start.5 = (s32[16,16]{1,0:T(8,128)S(1)}, s32[16,16]{1,0:T(8,128)}, u32[]{:S(2)}) copy-start(s32[16,16]{1,0:T(8,128)} %pattern.1) | copy-start | bytes 3076
  7.5 0.7 %copy-start.6 = (s32[1,64]{1,0:T(1,128)S(1)}, s32[1,64]{1,0:T(1,128)}, u32[]{:S(2)}) copy-start(s32[1,64]{1,0:T(1,128)} %ids.1) | copy-start | bytes 772

commit v2 on v1

--- a/solution.py
+++ b/solution.py
@@ -298,7 +298,7 @@
     rhs, sep_lower, sep_pattern, diag_inverse, child_lower, child_ids, child_count, child_x
 ):
     smem = pl.BlockSpec(memory_space=pltpu.SMEM)
-    hbm = pl.BlockSpec(memory_space=pl.ANY)
+    hbm = pl.BlockSpec(memory_space=pltpu.HBM)
     dma = pltpu.SemaphoreType.DMA
     found = pl.pallas_call(
         kernel,
@@ -334,7 +334,7 @@
             dma((CHIPS,)),
         ],
         compiler_params=pltpu.CompilerParams(
-            collective_id=0, has_side_effects=True, vmem_limit_bytes=48 * 2**20
+            collective_id=0, has_side_effects=True, vmem_limit_bytes=60 * 2**20
         ),
     )(
         sep_pattern, child_ids, child_count, rhs, sep_lower, diag_inverse, child_lower,

time: 42.5 us -> 37.2 us (0.88)
  local copies, waits for them, and re-layouts: 8.25 us -> 1.57 us
  Pallas kernels: 33.1 us -> 34.6 us
    unnamed x14 -> x0, local copies, waits for them, and re-layouts: 7.51 us -> none
    pallas_call x1, Pallas kernels: 33.1 us -> 34.6 us  [on_device(): pl.pallas_call(kernel, out_shape=jax.ShapeDtypeStruct((WIDTH, BS), BF16),...]
    transpose x1, local copies, waits for them, and re-layouts: 0.74 us -> 1.57 us  [on_device(): return found.T]
where the time goes in v2:
time: 37.2 us; the launch traced here: 36.8 us
  Pallas kernels  34.6 us (93%)
  local copies, waits for them, and re-layouts  1.57 us (4%)
  between operations  0.66 us (2%)
    pallas_call x1, Pallas kernels, on_device(): pl.pallas_call(kernel, out_shape=jax.ShapeDtypeStruct((WIDTH, BS), BF16),...  34.6 us
    transpose x1, local copies, waits for them, and re-layouts, on_device(): return found.T  1.57 us

profile of v2, /device:TPU:24, one launch (start us, length us, event | category | flops | bytes accessed | tf_op | source)
XLA Modules:
  0.0 36.8 jit_solution(14117749601789701197)
XLA Ops:
  0.7 34.6 %shard_map.82 = bf16[256,128]{1,0:T(8,128)(2,1)} custom-call(s32[16,16]{1,0:T(8,128)} %pattern.1, s32[1,64]{1,0:T(1,128)} %ids.1, s32[1,1]{1,0:T(1,128)S(6)} %copy.10.count, f32[128,256]{1,0:T(8,128)} %rhs_hbm.1, bf16[128,2048]{1,0:T(8,128)(2,1)} %sep_hbm.1, bf16[2048,128]{1,0:T(8,128)(2,1)} %dinv_hbm.1, bf16[128,8192]{1,0:T(8,128)(2,1)} %lower_hbm.1, ...), custom_call_target="tpu_custom_call" | custom-call | tf_op jit(solution)/shard_map/pallas_call | solution.py:303
  35.2 1.6 %copy.9 = bf16[128,256]{1,0:T(8,128)(2,1)} copy(bf16[128,256]{0,1:T(8,128)(2,1)} %bitcast.3) | data formatting | bytes 131072 | tf_op jit(solution)/shard_map/transpose | solution.py:343

commit v3 on v2

--- a/solution.py
+++ b/solution.py
@@ -28,8 +28,8 @@
 
 
 def kernel(
-    pattern, ids, count, rhs_hbm, sep_hbm, dinv_hbm, lower_hbm, x_hbm, out,
-    x_all, lower, sep, dinv, rhs, scaled, factor, relay, sums, parts, rhs_t,
+    pattern_hbm, ids_hbm, count_hbm, rhs_hbm, sep_hbm, dinv_hbm, lower_hbm, x_hbm, out,
+    pattern, ids, count, x_all, lower, sep, dinv, rhs, scaled, factor, relay, sums, parts, base,
     residual, residuals, solved, result,
     load_sem, factor_send, factor_recv, relay_sem, part_send, part_recv,
     residual_send, residual_recv, solved_send, result_send, result_recv,
@@ -49,16 +49,13 @@
 
     for step in FAR_FIRST:
         greet(row, 2 * other_chip(step))
-
-        @pl.when(first)
-        def _():
-            greet(row, 2 * other_chip(step) + 1)
+        greet(row, 2 * other_chip(step) + 1)
 
     greet(row, 2 * chip + 1 - core)
 
-    @pl.when(first & (row != LAST))
-    def _():
-        greet(LAST, col)
+    @pl.when(row != LAST)
+    def _():
+        greet(LAST, 2 * chip)
 
     @pl.when(solver)
     def _():
@@ -80,15 +77,21 @@
         return copy
 
     load_sep = load(sep_hbm, sep, 0)
+    load_small = [
+        load(src, dst, 4 + i)
+        for i, (src, dst) in enumerate([(pattern_hbm, pattern), (ids_hbm, ids), (count_hbm, count)])
+    ]
     load_dinv = load(dinv_hbm, dinv, 1)
     load_x = load(x_hbm, x_all.at[pl.ds(0, BLOCKS)], 2)
     span = SLOTS * BS // CHUNKS
     load_lower = [
-        load(lower_hbm.at[:, pl.ds(i * span, span)], lower.at[i], 4 + i) for i in range(CHUNKS)
+        load(lower_hbm.at[:, pl.ds(i * span, span)], lower.at[i], 7 + i) for i in range(CHUNKS)
     ]
     load_rhs = load(rhs_hbm, rhs, 3)
     x_all[BLOCKS] = jnp.zeros((BS, WIDTH), BF16)
 
+    for copy in load_small:
+        copy.wait()
     load_sep.wait()
     load_dinv.wait()
 
@@ -113,14 +116,14 @@
                 jnp.concatenate(picked, 0),
                 preferred_element_type=F32,
             )
-    sums[...] = total.T.reshape(CHIPS, PART, BS)
+    sums[...] = total.T.reshape(CHIPS, PART, BS).astype(BF16)
     load_rhs.wait()
-    rhs_t[...] = rhs[...].T.reshape(CHIPS, PART, BS)
+    base[...] = (rhs[...] - total).T.reshape(CHIPS, PART, BS)
 
     via_count = jnp.where((row == 10) | (row == 14), 1, 0)
     pl.semaphore_wait(
         barrier,
-        jnp.where(first, COLS - 1 + jnp.where(row == LAST, LAST, 1) + via_count, CHIPS),
+        COLS - 1 + jnp.where(first, jnp.where(row == LAST, 2 * LAST, 1) + via_count, 0),
     )
 
     def factor_copy(r):
@@ -166,37 +169,37 @@
             send_sem=residual_send.at[0], recv_sem=residual_recv.at[row],
             device_id=(LAST, col), device_id_type=MESH)
 
-    def result_copy(step, to_core):
+    def result_copy(step):
         return pltpu.make_async_remote_copy(
             src_ref=result.at[chip], dst_ref=result.at[chip],
-            send_sem=result_send.at[step, to_core], recv_sem=result_recv.at[chip],
-            device_id=(row, 2 * other_chip(step) + to_core), device_id_type=MESH)
-
-    def solved_copy(r):
+            send_sem=result_send.at[step], recv_sem=result_recv.at[chip],
+            device_id=(row, 2 * other_chip(step) + core), device_id_type=MESH)
+
+    def solved_copy(r, to_core):
         return pltpu.make_async_remote_copy(
             src_ref=solved.at[r], dst_ref=result.at[chip],
-            send_sem=solved_send.at[r], recv_sem=result_recv.at[chip],
-            device_id=(r, col), device_id_type=MESH)
+            send_sem=solved_send.at[r, to_core], recv_sem=result_recv.at[chip],
+            device_id=(r, 2 * chip + to_core), device_id_type=MESH)
 
     def result_wait(at):
         pltpu.make_async_remote_copy(
             src_ref=solved.at[0], dst_ref=result.at[at],
-            send_sem=result_send.at[0, 0], recv_sem=result_recv.at[at],
+            send_sem=result_send.at[0], recv_sem=result_recv.at[at],
             device_id=(row, col), device_id_type=MESH).wait_recv()
 
     @pl.when(first)
     def _():
-        parts[col] = sums[chip]
+        parts[col] = jnp.zeros((PART, BS), BF16)
         for k in range(1, COLS):
             src = lax.rem(col + k, COLS)
             pltpu.make_async_remote_copy(
                 src_ref=sums.at[0], dst_ref=parts.at[src],
                 send_sem=part_send.at[0], recv_sem=part_recv.at[src],
                 device_id=(row, col), device_id_type=MESH).wait_recv()
-        summed = parts[0]
-        for k in range(1, COLS):
-            summed += parts[k]
-        value = (rhs_t[chip] - summed).astype(BF16)
+        value = base[chip]
+        for k in range(COLS):
+            value -= parts[k].astype(F32)
+        value = value.astype(BF16)
 
         @pl.when(row != LAST)
         def _():
@@ -218,47 +221,43 @@
 
     @pl.when(solver)
     def _():
+        for r in range(LAST):
+            pltpu.make_async_remote_copy(
+                src_ref=residual, dst_ref=residuals.at[r],
+                send_sem=residual_send.at[0], recv_sem=residual_recv.at[r],
+                device_id=(LAST, col), device_id_type=MESH).wait_recv()
+        start = [dot_t(residuals[r], dinv[r * BS:(r + 1) * BS, :]) for r in range(ROWS)]
+        for r in range(1, LAST):
+            pltpu.make_async_remote_copy(
+                src_ref=scaled.at[pl.ds(0, r)], dst_ref=factor.at[r, pl.ds(0, r)],
+                send_sem=factor_send.at[0], recv_sem=factor_recv.at[r],
+                device_id=(LAST, col), device_id_type=MESH).wait_recv()
         done = []
         for r in range(ROWS):
-            if r < LAST:
-                pltpu.make_async_remote_copy(
-                    src_ref=residual, dst_ref=residuals.at[r],
-                    send_sem=residual_send.at[0], recv_sem=residual_recv.at[r],
-                    device_id=(LAST, col), device_id_type=MESH).wait_recv()
-            if 0 < r < LAST:
-                pltpu.make_async_remote_copy(
-                    src_ref=scaled.at[pl.ds(0, r)], dst_ref=factor.at[r, pl.ds(0, r)],
-                    send_sem=factor_send.at[0], recv_sem=factor_recv.at[r],
-                    device_id=(LAST, col), device_id_type=MESH).wait_recv()
-            block = dot_t(residuals[r], dinv[r * BS:(r + 1) * BS, :])
+            block = start[r]
+            blocks = [factor[r, j] if r < LAST else scaled[j] for j in range(r)]
+            if r > 1:
+                block -= dot_t(jnp.concatenate(done[:-1], 1), jnp.concatenate(blocks[:-1], 1))
             if r:
-                blocks = [factor[r, j] if r < LAST else scaled[j] for j in range(r)]
-                block -= dot_t(jnp.concatenate(done, 1), jnp.concatenate(blocks, 1))
+                block -= dot_t(done[-1], blocks[-1])
             block = block.astype(BF16)
             done.append(block)
+            solved[r] = block
             if r < LAST:
-                solved[r] = block
-                solved_copy(r).start()
+                for to_core in range(2):
+                    solved_copy(r, to_core).start()
             else:
+                solved_copy(r, 1).start()
                 result[chip] = block
 
-    @pl.when(first)
-    def _():
-        @pl.when(row != LAST)
-        def _():
-            result_wait(chip)
-
-        for step in FAR_FIRST:
-            for to_core in range(2):
-                result_copy(step, to_core).start()
-        result_copy(0, 1).start()
-
+    @pl.when(jnp.logical_not(solver))
+    def _():
+        result_wait(chip)
+
+    for step in FAR_FIRST:
+        result_copy(step).start()
     for step in range(1, CHIPS):
         result_wait(other_chip(step))
-
-    @pl.when(jnp.logical_not(first))
-    def _():
-        result_wait(chip)
 
     out[...] = result[...].reshape(WIDTH, BS)
 
@@ -272,40 +271,38 @@
             relay_copy(r).wait_send()
     for step in FAR_FIRST:
         part_copy(step).wait_send()
+        result_copy(step).wait_send()
 
     @pl.when(jnp.logical_not(first))
     def _():
         part_copy(0).wait_send()
 
-    @pl.when(first)
-    def _():
-        @pl.when(row != LAST)
-        def _():
-            residual_copy().wait_send()
-
-        for step in FAR_FIRST:
+    @pl.when(first & (row != LAST))
+    def _():
+        residual_copy().wait_send()
+
+    @pl.when(solver)
+    def _():
+        for r in range(ROWS):
             for to_core in range(2):
-                result_copy(step, to_core).wait_send()
-        result_copy(0, 1).wait_send()
-
-    @pl.when(solver)
-    def _():
-        for r in range(LAST):
-            solved_copy(r).wait_send()
+                if r < LAST or to_core:
+                    solved_copy(r, to_core).wait_send()
 
 
 def on_device(
     rhs, sep_lower, sep_pattern, diag_inverse, child_lower, child_ids, child_count, child_x
 ):
-    smem = pl.BlockSpec(memory_space=pltpu.SMEM)
     hbm = pl.BlockSpec(memory_space=pltpu.HBM)
     dma = pltpu.SemaphoreType.DMA
     found = pl.pallas_call(
         kernel,
-        out_shape=jax.ShapeDtypeStruct((WIDTH, BS), BF16),
-        in_specs=[smem] * 3 + [hbm] * 5,
+        out_shape=pltpu.VMEM((WIDTH, BS), BF16),
+        in_specs=[hbm] * 8,
         out_specs=pl.BlockSpec(memory_space=pltpu.VMEM),
         scratch_shapes=[
+            pltpu.SMEM((ROWS, ROWS), jnp.int32),
+            pltpu.SMEM((1, SLOTS), jnp.int32),
+            pltpu.SMEM((1, 1), jnp.int32),
             pltpu.VMEM((BLOCKS + 1, BS, WIDTH), BF16),
             pltpu.VMEM((CHUNKS, BS, SLOTS * BS // CHUNKS), BF16),
             pltpu.VMEM((BS, ROWS * BS), BF16),
@@ -314,14 +311,14 @@
             pltpu.VMEM((LAST, BS, BS), BF16),
             pltpu.VMEM((LAST, LAST - 1, BS, BS), BF16),
             pltpu.VMEM((10, BS, BS), BF16),
-            pltpu.VMEM((CHIPS, PART, BS), F32),
-            pltpu.VMEM((COLS, PART, BS), F32),
+            pltpu.VMEM((CHIPS, PART, BS), BF16),
+            pltpu.VMEM((COLS, PART, BS), BF16),
             pltpu.VMEM((CHIPS, PART, BS), F32),
             pltpu.VMEM((PART, BS), BF16),
             pltpu.VMEM((ROWS, PART, BS), BF16),
-            pltpu.VMEM((LAST, PART, BS), BF16),
+            pltpu.VMEM((ROWS, PART, BS), BF16),
             pltpu.VMEM((CHIPS, PART, BS), BF16),
-            dma((4 + CHUNKS,)),
+            dma((7 + CHUNKS,)),
             dma((1,)),
             dma((ROWS,)),
             dma((2,)),
@@ -329,8 +326,8 @@
             dma((COLS,)),
             dma((1,)),
             dma((ROWS,)),
-            dma((ROWS,)),
-            dma((CHIPS, 2)),
+            dma((ROWS, 2)),
+            dma((CHIPS,)),
             dma((CHIPS,)),
         ],
         compiler_params=pltpu.CompilerParams(

time: 37.2 us -> 35.4 us (0.952)
  local copies, waits for them, and re-layouts: 1.57 us -> 0.74 us
  Pallas kernels: 34.6 us -> 33.8 us
    transpose x1, local copies, waits for them, and re-layouts: 1.57 us -> 0.74 us  [on_device(): return found.T]
    pallas_call x1, Pallas kernels: 34.6 us -> 33.8 us  [on_device(): pl.pallas_call(kernel, out_shape=pltpu.VMEM((WIDTH, BS), BF16), in_specs=...]
where the time goes in v3:
time: 35.4 us; the launch traced here: 35.2 us
  Pallas kernels  33.8 us (95%)
  local copies, waits for them, and re-layouts  0.74 us (2%)
  between operations  0.66 us (2%)
    pallas_call x1, Pallas kernels, on_device(): pl.pallas_call(kernel, out_shape=pltpu.VMEM((WIDTH, BS), BF16), in_specs=...  33.8 us
    transpose x1, local copies, waits for them, and re-layouts, on_device(): return found.T  0.74 us

profile of v3, /device:TPU:24, one launch (start us, length us, event | category | flops | bytes accessed | tf_op | source)
XLA Modules:
  0.0 35.2 jit_solution(11486394293937956175)
XLA Ops:
  0.7 33.8 %shard_map.82 = bf16[256,128]{1,0:T(8,128)(2,1)S(1)} custom-call(s32[16,16]{1,0:T(8,128)} %pattern_hbm.1, s32[1,64]{1,0:T(1,128)} %ids_hbm.1, s32[1,1]{1,0:T(1,128)S(6)} %copy.10.count_hbm, f32[128,256]{1,0:T(8,128)} %rhs_hbm.1, bf16[128,2048]{1,0:T(8,128)(2,1)} %sep_hbm.1, bf16[2048,128]{1,0:T(8,128)(2,1)} %dinv_hbm.1, bf16[128,8192]{1,0:T(8,128)(2,1)} %lower_hbm.1, ...), custom_call_target="tpu_custom_call" | custom-call | tf_op jit(solution)/shard_map/pallas_call | solution.py:297
  34.5 0.7 %copy.9 = bf16[128,256]{1,0:T(8,128)(2,1)} copy(bf16[128,256]{0,1:T(8,128)(2,1)S(1)} %bitcast.2) | data formatting | bytes 131072 | tf_op jit(solution)/shard_map/transpose | solution.py:340

commit v4 on v3

v4 whole, which is shorter than its diff:
```python
import jax
import jax.numpy as jnp
from jax import lax
from jax.experimental import pallas as pl
from jax.experimental.pallas import tpu as pltpu
from jax.sharding import PartitionSpec as P

MESH = pl.DeviceIdType.MESH
BF16 = jnp.bfloat16
F32 = jnp.float32

ROWS = 16
COLS = 16
CHIPS = COLS // 2
SOLVERS = CHIPS // 2
BS = 128
WIDTH = 256
PART = WIDTH // SOLVERS
LAST = ROWS - 1
SLOTS = 64
BLOCKS = 32
CHUNKS = 4
FAR_FIRST = (4, 3, 5, 2, 6, 1, 7)

VIA = {12: [(4, 0, 4, 0), (5, 0, 5, 4)], 14: [(10, 0, 5, 0), (10, 5, 10, 5)]}
UP = [(11, 0, 4, 0), (11, 4, 8, 4), (11, 8, 11, 8)]
DOWN = [(12, 0, 4, 11), (12, 4, 8, 15), (12, 8, 12, 19)]
SIDE = sorted({piece[0] for piece in UP + DOWN})
ROUTED = {piece[0] for pieces in VIA.values() for piece in pieces} | set(SIDE)
STRAIGHT = [(r, 0, r, 0) for r in range(1, LAST) if r not in ROUTED]
PIECES = STRAIGHT + [piece for pieces in VIA.values() for piece in pieces] + UP + DOWN
RELAY_BLOCKS = 23


def dot_t(a, b):
    return lax.dot_general(a, b, (((1,), (1,)), ((), ())), preferred_element_type=F32)


def any_of(value, options):
    found = value == options[0]
    for option in options[1:]:
        found = found | (value == option)
    return found


def kernel(
    pattern_hbm, ids_hbm, count_hbm, rhs_hbm, sep_hbm, dinv_hbm, lower_hbm, x_hbm, out,
    pattern, ids, count, x_all, lower, sep, dinv, rhs, scaled, factor, relay, sums, parts, base,
    residual, residuals, solved, result,
    load_sem, factor_send, factor_recv, relay_send, relay_recv, part_send, part_recv,
    residual_send, residual_recv, solved_send, result_send, result_recv,
):
    row, col = lax.axis_index("row"), lax.axis_index("col")
    chip, core = col // 2, lax.rem(col, 2)
    mine = chip // 2
    even = lax.rem(chip, 2) == 0
    first = core == 0
    owner = first & even
    helper = even & (core == 1)
    solver = owner & (row == LAST)
    side = first & jnp.logical_not(even)

    def other_chip(step):
        return lax.rem(chip + step, CHIPS)

    barrier = pltpu.get_barrier_semaphore()

    def greet(r, c):
        pl.semaphore_signal(barrier, inc=1, device_id=(r, c), device_id_type=MESH)

    for step in FAR_FIRST:
        greet(row, 2 * other_chip(step))
        greet(row, 2 * other_chip(step) + 1)
    greet(row, 2 * chip + 1 - core)

    @pl.when(even & (row != LAST))
    def _():
        greet(LAST, 2 * chip)

    @pl.when(solver)
    def _():
        for r in range(LAST):
            greet(r, col)
        for via in VIA:
            greet(via, 2 * chip + 1)

    @pl.when(side & (row == LAST))
    def _():
        for r in SIDE:
            greet(r, col)

    for via, pieces in VIA.items():
        @pl.when(helper & (row == via))
        def _():
            for r in sorted({piece[0] for piece in pieces}):
                greet(r, 2 * chip)

    def load(src, dst, sem):
        copy = pltpu.make_async_copy(src, dst, load_sem.at[sem])
        copy.start()
        return copy

    load_sep = load(sep_hbm, sep, 0)
    load_dinv = load(dinv_hbm, dinv, 1)
    load_x = load(x_hbm, x_all.at[pl.ds(0, BLOCKS)], 2)
    load_small = [
        load(src, dst, 4 + i)
        for i, (src, dst) in enumerate([(pattern_hbm, pattern), (ids_hbm, ids), (count_hbm, count)])
    ]
    span = SLOTS * BS // CHUNKS
    load_lower = [
        load(lower_hbm.at[:, pl.ds(i * span, span)], lower.at[i], 7 + i) for i in range(CHUNKS)
    ]
    load_rhs = load(rhs_hbm, rhs, 3)
    x_all[BLOCKS] = jnp.zeros((BS, WIDTH), BF16)
    for copy in load_small:
        copy.wait()

    load_sep.wait()
    load_dinv.wait()

    @pl.when(first)
    def _():
        own = dinv[pl.ds(pl.multiple_of(row * BS, BS), BS), :]
        for j in range(LAST):
            term = jnp.dot(own, sep[:, j * BS:(j + 1) * BS], preferred_element_type=F32)
            scaled[j] = (term * pattern[row, j].astype(F32)).astype(BF16)

    load_x.wait()
    live = count[0, 0]
    total = jnp.zeros((BS, WIDTH), F32)
    pairs = SLOTS // 2 // CHUNKS
    for i in range(CHUNKS):
        load_lower[i].wait()
        for p in range(pairs):
            j = 2 * (i * pairs + p)
            picked = [x_all[jnp.where(s < live, ids[0, s], BLOCKS)] for s in (j, j + 1)]
            total += jnp.dot(
                lower[i, :, 2 * p * BS:2 * (p + 1) * BS],
                jnp.concatenate(picked, 0),
                preferred_element_type=F32,
            )
    sums[...] = total.T.reshape(SOLVERS, PART, BS).astype(BF16)
    load_rhs.wait()
    base[...] = (rhs[...] - total).T.reshape(SOLVERS, PART, BS)

    plane = jnp.where(row == LAST, 2 * LAST, 1)
    for via, pieces in VIA.items():
        plane += jnp.where(any_of(row, sorted({piece[0] for piece in pieces})), 1, 0)
    greeted = jnp.where(owner, plane, 0) + jnp.where(side & any_of(row, SIDE), 1, 0)
    greeted += jnp.where(helper & any_of(row, list(VIA)), 1, 0)
    pl.semaphore_wait(barrier, COLS - 1 + greeted)

    def straight_copy(piece):
        r, lo, hi, _ = piece
        i = PIECES.index(piece)
        return pltpu.make_async_remote_copy(
            src_ref=scaled.at[pl.ds(lo, hi - lo)], dst_ref=factor.at[r, pl.ds(lo, hi - lo)],
            send_sem=factor_send.at[i], recv_sem=factor_recv.at[i],
            device_id=(LAST, col), device_id_type=MESH)

    def first_leg(piece, via, to_core=0):
        _, lo, hi, at = piece
        i = PIECES.index(piece)
        return pltpu.make_async_remote_copy(
            src_ref=scaled.at[pl.ds(lo, hi - lo)], dst_ref=relay.at[pl.ds(at, hi - lo)],
            send_sem=factor_send.at[i], recv_sem=relay_recv.at[i],
            device_id=(via, 2 * chip + to_core), device_id_type=MESH)

    def second_leg(piece, to):
        r, lo, hi, at = piece
        i = PIECES.index(piece)
        return pltpu.make_async_remote_copy(
            src_ref=relay.at[pl.ds(at, hi - lo)], dst_ref=factor.at[r, pl.ds(lo, hi - lo)],
            send_sem=relay_send.at[i], recv_sem=factor_recv.at[i],
            device_id=(LAST, 2 * other_chip(to)), device_id_type=MESH)

    def pass_on(piece, to):
        first_leg(piece, LAST).wait_recv()
        second_leg(piece, to).start()

    for piece in STRAIGHT:
        @pl.when(owner & (row == piece[0]))
        def _():
            straight_copy(piece).start()

    for via, pieces in VIA.items():
        for piece in pieces:
            @pl.when(owner & (row == piece[0]))
            def _():
                first_leg(piece, via, 1).start()

    for piece in UP + DOWN:
        @pl.when(side & (row == piece[0]))
        def _():
            first_leg(piece, LAST).start()

    def part_copy(step):
        to = lax.rem(mine + step, SOLVERS)
        return pltpu.make_async_remote_copy(
            src_ref=sums.at[to], dst_ref=parts.at[col],
            send_sem=part_send.at[step], recv_sem=part_recv.at[col],
            device_id=(row, 4 * to), device_id_type=MESH)

    for step in (2, 3, 1):
        part_copy(step).start()

    @pl.when(jnp.logical_not(owner))
    def _():
        part_copy(0).start()

    def residual_copy():
        return pltpu.make_async_remote_copy(
            src_ref=residual, dst_ref=residuals.at[row],
            send_sem=residual_send.at[0], recv_sem=residual_recv.at[row],
            device_id=(LAST, col), device_id_type=MESH)

    def result_copy(step):
        return pltpu.make_async_remote_copy(
            src_ref=result.at[mine], dst_ref=result.at[mine],
            send_sem=result_send.at[step], recv_sem=result_recv.at[mine],
            device_id=(row, 2 * other_chip(step) + core), device_id_type=MESH)

    def solved_copy(r, to_core):
        return pltpu.make_async_remote_copy(
            src_ref=solved.at[r], dst_ref=result.at[mine],
            send_sem=solved_send.at[r, to_core], recv_sem=result_recv.at[mine],
            device_id=(r, 2 * chip + to_core), device_id_type=MESH)

    def result_wait(at):
        pltpu.make_async_remote_copy(
            src_ref=solved.at[0], dst_ref=result.at[at],
            send_sem=result_send.at[0], recv_sem=result_recv.at[at],
            device_id=(row, col), device_id_type=MESH).wait_recv()

    @pl.when(side & (row == LAST))
    def _():
        for up, down in zip(UP, DOWN):
            pass_on(up, CHIPS - 1)
            pass_on(down, 1)

    for via, pieces in VIA.items():
        @pl.when(helper & (row == via))
        def _():
            for piece in pieces:
                pass_on(piece, 0)

    @pl.when(owner)
    def _():
        parts[col] = jnp.zeros((PART, BS), BF16)
        for k in range(1, COLS):
            src = lax.rem(col + k, COLS)
            pltpu.make_async_remote_copy(
                src_ref=sums.at[0], dst_ref=parts.at[src],
                send_sem=part_send.at[0], recv_sem=part_recv.at[src],
                device_id=(row, col), device_id_type=MESH).wait_recv()
        value = base[mine]
        for k in range(COLS):
            value -= parts[k].astype(F32)
        value = value.astype(BF16)

        @pl.when(row != LAST)
        def _():
            residual[...] = value
            residual_copy().start()

        @pl.when(row == LAST)
        def _():
            residuals[LAST] = value

    @pl.when(solver)
    def _():
        for r in range(LAST):
            pltpu.make_async_remote_copy(
                src_ref=residual, dst_ref=residuals.at[r],
                send_sem=residual_send.at[0], recv_sem=residual_recv.at[r],
                device_id=(LAST, col), device_id_type=MESH).wait_recv()
        start = [dot_t(residuals[r], dinv[r * BS:(r + 1) * BS, :]) for r in range(ROWS)]
        done = []
        for r in range(ROWS):
            for piece in PIECES:
                if piece[0] == r:
                    straight_copy(piece).wait_recv()
            block = start[r]
            blocks = [factor[r, j] if r < LAST else scaled[j] for j in range(r)]
            if r > 1:
                block -= dot_t(jnp.concatenate(done[:-1], 1), jnp.concatenate(blocks[:-1], 1))
            if r:
                block -= dot_t(done[-1], blocks[-1])
            block = block.astype(BF16)
            done.append(block)
            solved[r] = block
            if r < LAST:
                for to_core in range(2):
                    solved_copy(r, to_core).start()
            else:
                solved_copy(r, 1).start()
                result[mine] = block

    @pl.when(even)
    def _():
        @pl.when(jnp.logical_not(solver))
        def _():
            result_wait(mine)

        for step in FAR_FIRST:
            result_copy(step).start()

    for step in range(1, SOLVERS):
        result_wait(lax.rem(mine + step, SOLVERS))

    @pl.when(jnp.logical_not(even))
    def _():
        result_wait(mine)

    out[...] = result[...].reshape(WIDTH, BS)

    for piece in STRAIGHT:
        @pl.when(owner & (row == piece[0]))
        def _():
            straight_copy(piece).wait_send()

    for via, pieces in VIA.items():
        for piece in pieces:
            @pl.when(owner & (row == piece[0]))
            def _():
                first_leg(piece, via, 1).wait_send()

            @pl.when(helper & (row == via))
            def _():
                second_leg(piece, 0).wait_send()

    for piece in UP + DOWN:
        @pl.when(side & (row == piece[0]))
        def _():
            first_leg(piece, LAST).wait_send()

        @pl.when(side & (row == LAST))
        def _():
            second_leg(piece, 1).wait_send()

    for step in (2, 3, 1):
        part_copy(step).wait_send()

    @pl.when(jnp.logical_not(owner))
    def _():
        part_copy(0).wait_send()

    @pl.when(even)
    def _():
        for step in FAR_FIRST:
            result_copy(step).wait_send()

    @pl.when(owner & (row != LAST))
    def _():
        residual_copy().wait_send()

    @pl.when(solver)
    def _():
        for r in range(ROWS):
            for to_core in range(2):
                if r < LAST or to_core:
                    solved_copy(r, to_core).wait_send()


def on_device(
    rhs, sep_lower, sep_pattern, diag_inverse, child_lower, child_ids, child_count, child_x
):
    dma = pltpu.SemaphoreType.DMA
    found = pl.pallas_call(
        kernel,
        out_shape=pltpu.VMEM((WIDTH, BS), BF16),
        in_specs=[pl.BlockSpec(memory_space=pltpu.HBM)] * 8,
        out_specs=pl.BlockSpec(memory_space=pltpu.VMEM),
        scratch_shapes=[
            pltpu.SMEM((ROWS, ROWS), jnp.int32),
            pltpu.SMEM((1, SLOTS), jnp.int32),
            pltpu.SMEM((1, 1), jnp.int32),
            pltpu.VMEM((BLOCKS + 1, BS, WIDTH), BF16),
            pltpu.VMEM((CHUNKS, BS, SLOTS * BS // CHUNKS), BF16),
            pltpu.VMEM((BS, ROWS * BS), BF16),
            pltpu.VMEM((ROWS * BS, BS), BF16),
            pltpu.VMEM((BS, WIDTH), F32),
            pltpu.VMEM((LAST, BS, BS), BF16),
            pltpu.VMEM((LAST, LAST - 1, BS, BS), BF16),
            pltpu.VMEM((RELAY_BLOCKS, BS, BS), BF16),
            pltpu.VMEM((SOLVERS, PART, BS), BF16),
            pltpu.VMEM((COLS, PART, BS), BF16),
            pltpu.VMEM((SOLVERS, PART, BS), F32),
            pltpu.VMEM((PART, BS), BF16),
            pltpu.VMEM((ROWS, PART, BS), BF16),
            pltpu.VMEM((ROWS, PART, BS), BF16),
            pltpu.VMEM((SOLVERS, PART, BS), BF16),
            dma((7 + CHUNKS,)),
            dma((len(PIECES),)),
            dma((len(PIECES),)),
            dma((len(PIECES),)),
            dma((len(PIECES),)),
            dma((SOLVERS,)),
            dma((COLS,)),
            dma((1,)),
            dma((ROWS,)),
            dma((ROWS, 2)),
            dma((CHIPS,)),
            dma((SOLVERS,)),
        ],
        compiler_params=pltpu.CompilerParams(
            collective_id=0, has_side_effects=True, vmem_limit_bytes=60 * 2**20
        ),
    )(
        sep_pattern, child_ids, child_count, rhs, sep_lower, diag_inverse, child_lower,
        child_x.reshape(BLOCKS, BS, WIDTH),
    )
    return found.T


def solution(mesh):
    in_specs = (
        P("row", None),
        P("row", None),
        P(),
        P(),
        P("row", "col"),
        P("row", "col"),
        P("row", "col"),
        P("col", None),
    )
    return jax.shard_map(
        on_device, mesh=mesh, in_specs=in_specs, out_specs=P("row", None), check_vma=False
    )
```

time: 35.4 us -> 34.1 us (0.963)
  Pallas kernels: 33.8 us -> 32.6 us
    pallas_call x1, Pallas kernels: 33.8 us -> 32.6 us  [on_device(): pl.pallas_call(kernel, out_shape=pltpu.VMEM((WIDTH, BS), BF16), in_specs=...]
where the time goes in v4:
time: 34.1 us; the launch traced here: 34 us
  Pallas kernels  32.6 us (96%)
  local copies, waits for them, and re-layouts  0.74 us (2%)
  between operations  0.66 us (2%)
    pallas_call x1, Pallas kernels, on_device(): pl.pallas_call(kernel, out_shape=pltpu.VMEM((WIDTH, BS), BF16), in_specs=...  32.6 us
    transpose x1, local copies, waits for them, and re-layouts, on_device(): return found.T  0.74 us

profile of v4, /device:TPU:24, one launch (start us, length us, event | category | flops | bytes accessed | tf_op | source)
XLA Modules:
  0.0 34.0 jit_solution(8751700696480956667)
XLA Ops:
  0.7 32.6 %shard_map.82 = bf16[256,128]{1,0:T(8,128)(2,1)S(1)} custom-call(s32[16,16]{1,0:T(8,128)} %pattern_hbm.1, s32[1,64]{1,0:T(1,128)} %ids_hbm.1, s32[1,1]{1,0:T(1,128)S(6)} %copy.10.count_hbm, f32[128,256]{1,0:T(8,128)} %rhs_hbm.1, bf16[128,2048]{1,0:T(8,128)(2,1)} %sep_hbm.1, bf16[2048,128]{1,0:T(8,128)(2,1)} %dinv_hbm.1, bf16[128,8192]{1,0:T(8,128)(2,1)} %lower_hbm.1, ...), custom_call_target="tpu_custom_call" | custom-call | tf_op jit(solution)/shard_map/pallas_call | solution.py:370
  33.2 0.7 %copy.9 = bf16[128,256]{1,0:T(8,128)(2,1)} copy(bf16[128,256]{0,1:T(8,128)(2,1)S(1)} %bitcast.2) | data formatting | bytes 131072 | tf_op jit(solution)/shard_map/transpose | solution.py:414

commit v5 on v4

v5 whole, which is shorter than its diff:
```python
import jax
import jax.numpy as jnp
from jax import lax
from jax.experimental import pallas as pl
from jax.experimental.pallas import tpu as pltpu
from jax.sharding import PartitionSpec as P

MESH = pl.DeviceIdType.MESH
BF16 = jnp.bfloat16
F32 = jnp.float32

ROWS = 16
COLS = 16
CHIPS = COLS // 2
SOLVERS = CHIPS // 2
BS = 128
WIDTH = 256
PART = WIDTH // SOLVERS
LAST = ROWS - 1
EARLY = 2
SLOTS = 64
BLOCKS = 32
CHUNKS = 4
FAR_FIRST = (4, 3, 5, 2, 6, 1, 7)

VIA = {12: [(8, 0, 4, 0), (8, 4, 8, 4)], 14: [(10, 0, 5, 0), (10, 5, 10, 5)]}
UP = [(6, 0, 2, 0), (6, 2, 4, 2), (6, 4, 6, 4), (12, 0, 3, 6), (12, 3, 6, 9)]
DOWN = [(7, 0, 2, 12), (7, 2, 4, 14), (7, 4, 7, 16), (12, 6, 9, 19), (12, 9, 12, 22)]
SIDE = sorted({piece[0] for piece in UP + DOWN})
ROUTED = {piece[0] for pieces in VIA.values() for piece in pieces} | set(SIDE)
STRAIGHT = [(r, 0, r, 0) for r in range(1, LAST) if r not in ROUTED]
PIECES = STRAIGHT + [piece for pieces in VIA.values() for piece in pieces] + UP + DOWN
RELAY_BLOCKS = 40
GROUPS = (range(0, 4), range(4, 8), range(8, 12), range(12, 16))


def dot_t(a, b):
    return lax.dot_general(a, b, (((1,), (1,)), ((), ())), preferred_element_type=F32)


def any_of(value, options):
    found = value == options[0]
    for option in options[1:]:
        found = found | (value == option)
    return found


def kernel(
    pattern_hbm, ids_hbm, count_hbm, rhs_hbm, sep_hbm, dinv_hbm, lower_hbm, x_hbm, out,
    pattern, ids, count, x_all, lower, sep, dinv, rhs, scaled, factor, relay, own_sum, given, sums,
    parts, base,
    residual, residuals, solved, result,
    load_sem, factor_send, factor_recv, relay_send, relay_recv, give_send, give_recv, part_send, part_recv,
    residual_send, residual_recv, solved_send, result_send, result_recv,
):
    row, col = lax.axis_index("row"), lax.axis_index("col")
    chip, core = col // 2, lax.rem(col, 2)
    mine = chip // 2
    even = lax.rem(chip, 2) == 0
    first = core == 0
    owner = first & even
    reducer = even & (core == 1)
    solver = owner & (row == LAST)
    side = first & jnp.logical_not(even)

    def other_chip(step):
        return lax.rem(chip + step, CHIPS)

    barrier = pltpu.get_barrier_semaphore()

    def greet(r, c):
        pl.semaphore_signal(barrier, inc=1, device_id=(r, c), device_id_type=MESH)

    @pl.when(first)
    def _():
        for step in (2, 3, 1, 0):
            greet(row, 4 * lax.rem(mine + step, SOLVERS) + 1)

        @pl.when(solver)
        def _():
            for r in range(LAST):
                greet(r, col)
            for r in range(ROWS):
                greet(r, 2 * chip + 1)
            for step in (1, CHIPS - 1):
                greet(LAST, 2 * other_chip(step))

        @pl.when(side & (row == LAST))
        def _():
            for r in SIDE:
                greet(r, col)

        for via, pieces in VIA.items():
            @pl.when(owner & (row == via))
            def _():
                for r in sorted({piece[0] for piece in pieces}):
                    greet(r, col)

    @pl.when(core == 1)
    def _():
        greet(row, 2 * chip)

        @pl.when(even)
        def _():
            for step in FAR_FIRST:
                greet(row, 2 * other_chip(step) + 1)
            greet(LAST, 2 * chip)

        @pl.when(jnp.logical_not(even))
        def _():
            for step in (3, 5, 1, 7):
                greet(row, 2 * other_chip(step) + 1)

    def load(src, dst, sem):
        copy = pltpu.make_async_copy(src, dst, load_sem.at[sem])
        copy.start()
        return copy

    load_sep = load(sep_hbm, sep, 0)
    load_dinv = load(dinv_hbm, dinv, 1)
    load_x = load(x_hbm, x_all.at[pl.ds(0, BLOCKS)], 2)
    load_small = [
        load(src, dst, 4 + i)
        for i, (src, dst) in enumerate([(pattern_hbm, pattern), (ids_hbm, ids), (count_hbm, count)])
    ]
    span = SLOTS * BS // CHUNKS
    load_lower = [
        load(lower_hbm.at[:, pl.ds(i * span, span)], lower.at[i], 7 + i) for i in range(CHUNKS)
    ]
    load_rhs = load(rhs_hbm, rhs, 3)
    x_all[BLOCKS] = jnp.zeros((BS, WIDTH), BF16)
    for copy in load_small:
        copy.wait()

    load_sep.wait()
    load_dinv.wait()

    @pl.when(first)
    def _():
        own = dinv[pl.ds(pl.multiple_of(row * BS, BS), BS), :]
        for j in range(LAST):
            term = jnp.dot(own, sep[:, j * BS:(j + 1) * BS], preferred_element_type=F32)
            scaled[j] = (term * pattern[row, j].astype(F32)).astype(BF16)

    def straight_copy(piece):
        r, lo, hi, _ = piece
        i = PIECES.index(piece)
        return pltpu.make_async_remote_copy(
            src_ref=scaled.at[pl.ds(lo, hi - lo)], dst_ref=factor.at[r, pl.ds(lo, hi - lo)],
            send_sem=factor_send.at[i], recv_sem=factor_recv.at[i],
            device_id=(LAST, col), device_id_type=MESH)

    def first_leg(piece, via):
        _, lo, hi, at = piece
        i = PIECES.index(piece)
        return pltpu.make_async_remote_copy(
            src_ref=scaled.at[pl.ds(lo, hi - lo)], dst_ref=relay.at[pl.ds(at, hi - lo)],
            send_sem=factor_send.at[i], recv_sem=relay_recv.at[i],
            device_id=(via, col), device_id_type=MESH)

    def second_leg(piece, to):
        r, lo, hi, at = piece
        i = PIECES.index(piece)
        return pltpu.make_async_remote_copy(
            src_ref=relay.at[pl.ds(at, hi - lo)], dst_ref=factor.at[r, pl.ds(lo, hi - lo)],
            send_sem=relay_send.at[i], recv_sem=factor_recv.at[i],
            device_id=(LAST, 2 * other_chip(to)), device_id_type=MESH)

    def pass_on(piece, to):
        first_leg(piece, LAST).wait_recv()
        second_leg(piece, to).start()

    load_x.wait()
    live = count[0, 0]
    pairs = SLOTS // 2 // CHUNKS

    def child_sum(total, chunks):
        for i in chunks:
            load_lower[i].wait()
            for p in range(pairs):
                j = 2 * (i * pairs + p)
                picked = [x_all[jnp.where(s < live, ids[0, s], BLOCKS)] for s in (j, j + 1)]
                total += jnp.dot(
                    lower[i, :, 2 * p * BS:2 * (p + 1) * BS],
                    jnp.concatenate(picked, 0),
                    preferred_element_type=F32,
                )
        return total

    total = child_sum(jnp.zeros((BS, WIDTH), F32), range(EARLY))

    @pl.when(first)
    def _():
        greeted = 1 + jnp.where(even, jnp.where(row == LAST, ROWS, 1), 0)
        for via, pieces in VIA.items():
            greeted += jnp.where(even & any_of(row, sorted({piece[0] for piece in pieces})), 1, 0)
        greeted += jnp.where(side & any_of(row, SIDE), 1, 0)
        greeted += jnp.where(side & (row == LAST), 2, 0)
        pl.semaphore_wait(barrier, greeted)
        for piece in STRAIGHT:
            @pl.when(owner & (row == piece[0]))
            def _():
                straight_copy(piece).start()

        for via, pieces in VIA.items():
            for piece in pieces:
                @pl.when(owner & (row == piece[0]))
                def _():
                    first_leg(piece, via).start()

        for piece in UP + DOWN:
            @pl.when(side & (row == piece[0]))
            def _():
                first_leg(piece, LAST).start()

    total = child_sum(total, range(EARLY, CHUNKS))
    load_rhs.wait()

    def give_copy():
        return pltpu.make_async_remote_copy(
            src_ref=own_sum, dst_ref=given, send_sem=give_send.at[0], recv_sem=give_recv.at[0],
            device_id=(row, 2 * chip + 1), device_id_type=MESH)

    @pl.when(first)
    def _():
        own_sum[...] = total.T.reshape(SOLVERS, PART, BS)
        give_copy().start()

    @pl.when(core == 1)
    def _():
        own_sum[...] = total.T.reshape(SOLVERS, PART, BS)
        base[...] = rhs[...].T.reshape(SOLVERS, PART, BS)
        pl.semaphore_wait(barrier, jnp.where(even, 2 * CHIPS, SOLVERS))
        give_copy().wait_recv()
        both = own_sum[...] + given[...]
        sums[...] = both.astype(BF16)
        base[...] -= both

    def part_copy(step):
        to = lax.rem(mine + step, SOLVERS)
        return pltpu.make_async_remote_copy(
            src_ref=sums.at[to], dst_ref=parts.at[chip],
            send_sem=part_send.at[step], recv_sem=part_recv.at[chip],
            device_id=(row, 4 * to + 1), device_id_type=MESH)

    @pl.when(core == 1)
    def _():
        for step in (2, 3, 1):
            part_copy(step).start()

        @pl.when(jnp.logical_not(even))
        def _():
            part_copy(0).start()

    def residual_copy():
        return pltpu.make_async_remote_copy(
            src_ref=residual, dst_ref=residuals.at[row],
            send_sem=residual_send.at[0], recv_sem=residual_recv.at[row],
            device_id=(LAST, 2 * chip), device_id_type=MESH)

    def result_copy(step, to_core):
        return pltpu.make_async_remote_copy(
            src_ref=result.at[mine], dst_ref=result.at[mine],
            send_sem=result_send.at[step, to_core], recv_sem=result_recv.at[mine],
            device_id=(row, 2 * other_chip(step) + to_core), device_id_type=MESH)

    def solved_copy(r):
        return pltpu.make_async_remote_copy(
            src_ref=solved.at[r], dst_ref=result.at[mine],
            send_sem=solved_send.at[r], recv_sem=result_recv.at[mine],
            device_id=(r, 2 * chip + 1), device_id_type=MESH)

    def result_wait(at):
        pltpu.make_async_remote_copy(
            src_ref=solved.at[0], dst_ref=result.at[at],
            send_sem=result_send.at[0, 0], recv_sem=result_recv.at[at],
            device_id=(row, col), device_id_type=MESH).wait_recv()

    @pl.when(side & (row == LAST))
    def _():
        for i in range(max(len(UP), len(DOWN))):
            for piece in UP[i:i + 1]:
                pass_on(piece, CHIPS - 1)
            for piece in DOWN[i:i + 1]:
                pass_on(piece, 1)

    for via, pieces in VIA.items():
        @pl.when(owner & (row == via))
        def _():
            for piece in pieces:
                pass_on(piece, 0)

    @pl.when(reducer)
    def _():
        for k in range(1, CHIPS):
            src = other_chip(k)
            pltpu.make_async_remote_copy(
                src_ref=sums.at[0], dst_ref=parts.at[src],
                send_sem=part_send.at[0], recv_sem=part_recv.at[src],
                device_id=(row, col), device_id_type=MESH).wait_recv()
        value = base[mine]
        for k in range(1, CHIPS):
            value -= parts[other_chip(k)].astype(F32)
        residual[...] = value.astype(BF16)
        residual_copy().start()

    @pl.when(solver)
    def _():
        done = []
        for group in GROUPS:
            for r in group:
                pltpu.make_async_remote_copy(
                    src_ref=residual, dst_ref=residuals.at[r],
                    send_sem=residual_send.at[0], recv_sem=residual_recv.at[r],
                    device_id=(LAST, col), device_id_type=MESH).wait_recv()
                for piece in PIECES:
                    if piece[0] == r:
                        straight_copy(piece).wait_recv()
            blocks = {r: [factor[r, j] if r < LAST else scaled[j] for j in range(r)] for r in group}
            start = {r: dot_t(residuals[r], dinv[r * BS:(r + 1) * BS, :]) for r in group}
            top = group[0]
            if top:
                known = jnp.concatenate(done, 1)
                for r in group:
                    start[r] -= dot_t(known, jnp.concatenate(blocks[r][:top], 1))
            for r in group:
                block = start[r]
                if r - top > 1:
                    block -= dot_t(
                        jnp.concatenate(done[top:r - 1], 1), jnp.concatenate(blocks[r][top:r - 1], 1))
                if r > top:
                    block -= dot_t(done[r - 1], blocks[r][r - 1])
                block = block.astype(BF16)
                done.append(block)
                solved[r] = block
                solved_copy(r).start()

    @pl.when(reducer)
    def _():
        result_wait(mine)
        for step in FAR_FIRST:
            for to_core in (1, 0):
                result_copy(step, to_core).start()
        result_copy(0, 0).start()

    for step in range(1, SOLVERS):
        result_wait(lax.rem(mine + step, SOLVERS))

    @pl.when(jnp.logical_not(reducer))
    def _():
        result_wait(mine)

    out[...] = result[...].reshape(WIDTH, BS)

    for piece in STRAIGHT:
        @pl.when(owner & (row == piece[0]))
        def _():
            straight_copy(piece).wait_send()

    for via, pieces in VIA.items():
        for piece in pieces:
            @pl.when(owner & (row == piece[0]))
            def _():
                first_leg(piece, via).wait_send()

            @pl.when(owner & (row == via))
            def _():
                second_leg(piece, 0).wait_send()

    for piece in UP + DOWN:
        @pl.when(side & (row == piece[0]))
        def _():
            first_leg(piece, LAST).wait_send()

        @pl.when(side & (row == LAST))
        def _():
            second_leg(piece, 1).wait_send()

    @pl.when(first)
    def _():
        give_copy().wait_send()

    @pl.when(core == 1)
    def _():
        for step in (2, 3, 1):
            part_copy(step).wait_send()

        @pl.when(jnp.logical_not(even))
        def _():
            part_copy(0).wait_send()

    @pl.when(reducer)
    def _():
        residual_copy().wait_send()
        for step in FAR_FIRST:
            for to_core in (1, 0):
                result_copy(step, to_core).wait_send()
        result_copy(0, 0).wait_send()

    @pl.when(solver)
    def _():
        for r in range(ROWS):
            solved_copy(r).wait_send()


def on_device(
    rhs, sep_lower, sep_pattern, diag_inverse, child_lower, child_ids, child_count, child_x
):
    dma = pltpu.SemaphoreType.DMA
    found = pl.pallas_call(
        kernel,
        out_shape=pltpu.VMEM((WIDTH, BS), BF16),
        in_specs=[pl.BlockSpec(memory_space=pltpu.HBM)] * 8,
        out_specs=pl.BlockSpec(memory_space=pltpu.VMEM),
        scratch_shapes=[
            pltpu.SMEM((ROWS, ROWS), jnp.int32),
            pltpu.SMEM((1, SLOTS), jnp.int32),
            pltpu.SMEM((1, 1), jnp.int32),
            pltpu.VMEM((BLOCKS + 1, BS, WIDTH), BF16),
            pltpu.VMEM((CHUNKS, BS, SLOTS * BS // CHUNKS), BF16),
            pltpu.VMEM((BS, ROWS * BS), BF16),
            pltpu.VMEM((ROWS * BS, BS), BF16),
            pltpu.VMEM((BS, WIDTH), F32),
            pltpu.VMEM((LAST, BS, BS), BF16),
            pltpu.VMEM((LAST, LAST - 1, BS, BS), BF16),
            pltpu.VMEM((RELAY_BLOCKS, BS, BS), BF16),
            pltpu.VMEM((SOLVERS, PART, BS), F32),
            pltpu.VMEM((SOLVERS, PART, BS), F32),
            pltpu.VMEM((SOLVERS, PART, BS), BF16),
            pltpu.VMEM((CHIPS, PART, BS), BF16),
            pltpu.VMEM((SOLVERS, PART, BS), F32),
            pltpu.VMEM((PART, BS), BF16),
            pltpu.VMEM((ROWS, PART, BS), BF16),
            pltpu.VMEM((ROWS, PART, BS), BF16),
            pltpu.VMEM((SOLVERS, PART, BS), BF16),
            dma((7 + CHUNKS,)),
            dma((len(PIECES),)),
            dma((len(PIECES),)),
            dma((len(PIECES),)),
            dma((len(PIECES),)),
            dma((1,)),
            dma((1,)),
            dma((SOLVERS,)),
            dma((CHIPS,)),
            dma((1,)),
            dma((ROWS,)),
            dma((ROWS,)),
            dma((CHIPS, 2)),
            dma((SOLVERS,)),
        ],
        compiler_params=pltpu.CompilerParams(
            collective_id=0, has_side_effects=True, vmem_limit_bytes=60 * 2**20
        ),
    )(
        sep_pattern, child_ids, child_count, rhs, sep_lower, diag_inverse, child_lower,
        child_x.reshape(BLOCKS, BS, WIDTH),
    )
    return found.T


def solution(mesh):
    in_specs = (
        P("row", None),
        P("row", None),
        P(),
        P(),
        P("row", "col"),
        P("row", "col"),
        P("row", "col"),
        P("col", None),
    )
    return jax.shard_map(
        on_device, mesh=mesh, in_specs=in_specs, out_specs=P("row", None), check_vma=False
    )
```

time: 34.1 us -> 33 us (0.968)
  Pallas kernels: 32.6 us -> 31.6 us
    pallas_call x1, Pallas kernels: 32.6 us -> 31.6 us  [on_device(): pl.pallas_call(kernel, out_shape=pltpu.VMEM((WIDTH, BS), BF16), in_specs=...]
where the time goes in v5:
time: 33 us
  Pallas kernels  31.6 us (96%)
  local copies, waits for them, and re-layouts  0.74 us (2%)
  between operations  0.66 us (2%)
    pallas_call x1, Pallas kernels, on_device(): pl.pallas_call(kernel, out_shape=pltpu.VMEM((WIDTH, BS), BF16), in_specs=...  31.6 us
    transpose x1, local copies, waits for them, and re-layouts, on_device(): return found.T  0.74 us

profile of v5, /device:TPU:24, one launch (start us, length us, event | category | flops | bytes accessed | tf_op | source)
XLA Modules:
  0.0 33.0 jit_solution(6223239613172851470)
XLA Ops:
  0.7 31.6 %shard_map.82 = bf16[256,128]{1,0:T(8,128)(2,1)S(1)} custom-call(s32[16,16]{1,0:T(8,128)} %pattern_hbm.1, s32[1,64]{1,0:T(1,128)} %ids_hbm.1, s32[1,1]{1,0:T(1,128)S(6)} %copy.10.count_hbm, f32[128,256]{1,0:T(8,128)} %rhs_hbm.1, bf16[128,2048]{1,0:T(8,128)(2,1)} %sep_hbm.1, bf16[2048,128]{1,0:T(8,128)(2,1)} %dinv_hbm.1, bf16[128,8192]{1,0:T(8,128)(2,1)} %lower_hbm.1, ...), custom_call_target="tpu_custom_call" | custom-call | tf_op jit(solution)/shard_map/pallas_call | solution.py:410
  32.2 0.7 %copy.9 = bf16[128,256]{1,0:T(8,128)(2,1)} copy(bf16[128,256]{0,1:T(8,128)(2,1)S(1)} %bitcast.2) | data formatting | bytes 131072 | tf_op jit(solution)/shard_map/transpose | solution.py:458

commit v6 on v5

--- a/solution.py
+++ b/solution.py
@@ -23,15 +23,15 @@
 CHUNKS = 4
 FAR_FIRST = (4, 3, 5, 2, 6, 1, 7)
 
-VIA = {12: [(8, 0, 4, 0), (8, 4, 8, 4)], 14: [(10, 0, 5, 0), (10, 5, 10, 5)]}
-UP = [(6, 0, 2, 0), (6, 2, 4, 2), (6, 4, 6, 4), (12, 0, 3, 6), (12, 3, 6, 9)]
-DOWN = [(7, 0, 2, 12), (7, 2, 4, 14), (7, 4, 7, 16), (12, 6, 9, 19), (12, 9, 12, 22)]
+VIA = {12: [(8, 0, 4, 0), (8, 4, 8, 4)], 14: [(6, 0, 3, 0), (6, 3, 6, 3), (10, 5, 10, 6)]}
+UP = [(7, 0, 2, 0), (7, 2, 3, 2), (10, 0, 3, 3), (10, 3, 5, 6), (12, 0, 4, 8)]
+DOWN = [(7, 3, 5, 12), (7, 5, 7, 14), (12, 4, 8, 16), (12, 8, 12, 20)]
 SIDE = sorted({piece[0] for piece in UP + DOWN})
 ROUTED = {piece[0] for pieces in VIA.values() for piece in pieces} | set(SIDE)
 STRAIGHT = [(r, 0, r, 0) for r in range(1, LAST) if r not in ROUTED]
 PIECES = STRAIGHT + [piece for pieces in VIA.values() for piece in pieces] + UP + DOWN
 RELAY_BLOCKS = 40
-GROUPS = (range(0, 4), range(4, 8), range(8, 12), range(12, 16))
+GROUPS = (range(0, 4), range(4, 6), range(6, 8), range(8, 10), range(10, 12), range(12, 16))
 
 
 def dot_t(a, b):
@@ -279,10 +279,10 @@
     @pl.when(side & (row == LAST))
     def _():
         for i in range(max(len(UP), len(DOWN))):
+            for piece in DOWN[i:i + 1]:
+                pass_on(piece, 1)
             for piece in UP[i:i + 1]:
                 pass_on(piece, CHIPS - 1)
-            for piece in DOWN[i:i + 1]:
-                pass_on(piece, 1)
 
     for via, pieces in VIA.items():
         @pl.when(owner & (row == via))

time: 33 us -> 31.8 us (0.964)
  Pallas kernels: 31.6 us -> 30.3 us
    pallas_call x1, Pallas kernels: 31.6 us -> 30.3 us  [on_device(): pl.pallas_call(kernel, out_shape=pltpu.VMEM((WIDTH, BS), BF16), in_specs=...]
where the time goes in v6:
time: 31.8 us; the launch traced here: 31.7 us
  Pallas kernels  30.3 us (95%)
  local copies, waits for them, and re-layouts  0.74 us (2%)
  between operations  0.66 us (2%)
    pallas_call x1, Pallas kernels, on_device(): pl.pallas_call(kernel, out_shape=pltpu.VMEM((WIDTH, BS), BF16), in_specs=...  30.3 us
    transpose x1, local copies, waits for them, and re-layouts, on_device(): return found.T  0.74 us

profile of v6, /device:TPU:24, one launch (start us, length us, event | category | flops | bytes accessed | tf_op | source)
XLA Modules:
  0.0 31.7 jit_solution(17232415812588657659)
XLA Ops:
  0.7 30.3 %shard_map.82 = bf16[256,128]{1,0:T(8,128)(2,1)S(1)} custom-call(s32[16,16]{1,0:T(8,128)} %pattern_hbm.1, s32[1,64]{1,0:T(1,128)} %ids_hbm.1, s32[1,1]{1,0:T(1,128)S(6)} %copy.10.count_hbm, f32[128,256]{1,0:T(8,128)} %rhs_hbm.1, bf16[128,2048]{1,0:T(8,128)(2,1)} %sep_hbm.1, bf16[2048,128]{1,0:T(8,128)(2,1)} %dinv_hbm.1, bf16[128,8192]{1,0:T(8,128)(2,1)} %lower_hbm.1, ...), custom_call_target="tpu_custom_call" | custom-call | tf_op jit(solution)/shard_map/pallas_call | solution.py:410
  31.0 0.7 %copy.9 = bf16[128,256]{1,0:T(8,128)(2,1)} copy(bf16[128,256]{0,1:T(8,128)(2,1)S(1)} %bitcast.2) | data formatting | bytes 131072 | tf_op jit(solution)/shard_map/transpose | solution.py:458

commit v7 on v6

--- a/solution.py
+++ b/solution.py
@@ -23,12 +23,13 @@
 CHUNKS = 4
 FAR_FIRST = (4, 3, 5, 2, 6, 1, 7)
 
-VIA = {12: [(8, 0, 4, 0), (8, 4, 8, 4)], 14: [(6, 0, 3, 0), (6, 3, 6, 3), (10, 5, 10, 6)]}
+VIA = {12: [(8, 0, 4, 0), (8, 4, 8, 4)], 14: [(6, 0, 3, 0), (6, 3, 6, 3), (10, 5, 7, 6)]}
 UP = [(7, 0, 2, 0), (7, 2, 3, 2), (10, 0, 3, 3), (10, 3, 5, 6), (12, 0, 4, 8)]
 DOWN = [(7, 3, 5, 12), (7, 5, 7, 14), (12, 4, 8, 16), (12, 8, 12, 20)]
 SIDE = sorted({piece[0] for piece in UP + DOWN})
 ROUTED = {piece[0] for pieces in VIA.values() for piece in pieces} | set(SIDE)
 STRAIGHT = [(r, 0, r, 0) for r in range(1, LAST) if r not in ROUTED]
+STRAIGHT += [(10, 7, 10, 0)]
 PIECES = STRAIGHT + [piece for pieces in VIA.values() for piece in pieces] + UP + DOWN
 RELAY_BLOCKS = 40
 GROUPS = (range(0, 4), range(4, 6), range(6, 8), range(8, 10), range(10, 12), range(12, 16))
@@ -73,17 +74,14 @@
 
     @pl.when(first)
     def _():
-        for step in (2, 3, 1, 0):
-            greet(row, 4 * lax.rem(mine + step, SOLVERS) + 1)
-
         @pl.when(solver)
         def _():
-            for r in range(LAST):
+            for r in (5, 6, 9, 1, 4, 2, 7, 8, 10, 13, 3, 11, 14, 12, 0):
                 greet(r, col)
+            for step in (1, CHIPS - 1):
+                greet(LAST, 2 * other_chip(step))
             for r in range(ROWS):
                 greet(r, 2 * chip + 1)
-            for step in (1, CHIPS - 1):
-                greet(LAST, 2 * other_chip(step))
 
         @pl.when(side & (row == LAST))
         def _():
@@ -95,6 +93,9 @@
             def _():
                 for r in sorted({piece[0] for piece in pieces}):
                     greet(r, col)
+
+        for step in (2, 3, 1, 0):
+            greet(row, 4 * lax.rem(mine + step, SOLVERS) + 1)
 
     @pl.when(core == 1)
     def _():

time: 31.8 us -> 31.6 us (level)
  no operation moved by 1% of the time
where the time goes in v7:
time: 31.6 us; the launch traced here: 31.5 us
  Pallas kernels  30.1 us (95%)
  local copies, waits for them, and re-layouts  0.74 us (2%)
  between operations  0.66 us (2%)
    pallas_call x1, Pallas kernels, on_device(): pl.pallas_call(kernel, out_shape=pltpu.VMEM((WIDTH, BS), BF16), in_specs=...  30.1 us
    transpose x1, local copies, waits for them, and re-layouts, on_device(): return found.T  0.74 us

profile of v7, /device:TPU:24, one launch (start us, length us, event | category | flops | bytes accessed | tf_op | source)
XLA Modules:
  0.0 31.5 jit_solution(3055916585308116161)
XLA Ops:
  0.7 30.1 %shard_map.82 = bf16[256,128]{1,0:T(8,128)(2,1)S(1)} custom-call(s32[16,16]{1,0:T(8,128)} %pattern_hbm.1, s32[1,64]{1,0:T(1,128)} %ids_hbm.1, s32[1,1]{1,0:T(1,128)S(6)} %copy.10.count_hbm, f32[128,256]{1,0:T(8,128)} %rhs_hbm.1, bf16[128,2048]{1,0:T(8,128)(2,1)} %sep_hbm.1, bf16[2048,128]{1,0:T(8,128)(2,1)} %dinv_hbm.1, bf16[128,8192]{1,0:T(8,128)(2,1)} %lower_hbm.1, ...), custom_call_target="tpu_custom_call" | custom-call | tf_op jit(solution)/shard_map/pallas_call | solution.py:411
  30.8 0.7 %copy.9 = bf16[128,256]{1,0:T(8,128)(2,1)} copy(bf16[128,256]{0,1:T(8,128)(2,1)S(1)} %bitcast.2) | data formatting | bytes 131072 | tf_op jit(solution)/shard_map/transpose | solution.py:459

commit v8 on v7

--- a/solution.py
+++ b/solution.py
@@ -219,12 +219,12 @@
 
     def give_copy():
         return pltpu.make_async_remote_copy(
-            src_ref=own_sum, dst_ref=given, send_sem=give_send.at[0], recv_sem=give_recv.at[0],
+            src_ref=sums, dst_ref=given, send_sem=give_send.at[0], recv_sem=give_recv.at[0],
             device_id=(row, 2 * chip + 1), device_id_type=MESH)
 
     @pl.when(first)
     def _():
-        own_sum[...] = total.T.reshape(SOLVERS, PART, BS)
+        sums[...] = total.T.reshape(SOLVERS, PART, BS).astype(BF16)
         give_copy().start()
 
     @pl.when(core == 1)
@@ -233,7 +233,7 @@
         base[...] = rhs[...].T.reshape(SOLVERS, PART, BS)
         pl.semaphore_wait(barrier, jnp.where(even, 2 * CHIPS, SOLVERS))
         give_copy().wait_recv()
-        both = own_sum[...] + given[...]
+        both = own_sum[...] + given[...].astype(F32)
         sums[...] = both.astype(BF16)
         base[...] -= both
 
@@ -426,7 +426,7 @@
             pltpu.VMEM((LAST, LAST - 1, BS, BS), BF16),
             pltpu.VMEM((RELAY_BLOCKS, BS, BS), BF16),
             pltpu.VMEM((SOLVERS, PART, BS), F32),
-            pltpu.VMEM((SOLVERS, PART, BS), F32),
+            pltpu.VMEM((SOLVERS, PART, BS), BF16),
             pltpu.VMEM((SOLVERS, PART, BS), BF16),
             pltpu.VMEM((CHIPS, PART, BS), BF16),
             pltpu.VMEM((SOLVERS, PART, BS), F32),

time: 31.6 us -> 31.6 us (level)
  no operation moved by 1% of the time
where the time goes in v8:
time: 31.6 us; the launch traced here: 31.5 us
  Pallas kernels  30.1 us (95%)
  local copies, waits for them, and re-layouts  0.74 us (2%)
  between operations  0.66 us (2%)
    pallas_call x1, Pallas kernels, on_device(): pl.pallas_call(kernel, out_shape=pltpu.VMEM((WIDTH, BS), BF16), in_specs=...  30.1 us
    transpose x1, local copies, waits for them, and re-layouts, on_device(): return found.T  0.74 us

profile of v8, /device:TPU:24, one launch (start us, length us, event | category | flops | bytes accessed | tf_op | source)
XLA Modules:
  0.0 31.5 jit_solution(10595226971957980517)
XLA Ops:
  0.7 30.1 %shard_map.82 = bf16[256,128]{1,0:T(8,128)(2,1)S(1)} custom-call(s32[16,16]{1,0:T(8,128)} %pattern_hbm.1, s32[1,64]{1,0:T(1,128)} %ids_hbm.1, s32[1,1]{1,0:T(1,128)S(6)} %copy.10.count_hbm, f32[128,256]{1,0:T(8,128)} %rhs_hbm.1, bf16[128,2048]{1,0:T(8,128)(2,1)} %sep_hbm.1, bf16[2048,128]{1,0:T(8,128)(2,1)} %dinv_hbm.1, bf16[128,8192]{1,0:T(8,128)(2,1)} %lower_hbm.1, ...), custom_call_target="tpu_custom_call" | custom-call | tf_op jit(solution)/shard_map/pallas_call | solution.py:411
  30.8 0.7 %copy.9 = bf16[128,256]{1,0:T(8,128)(2,1)} copy(bf16[128,256]{0,1:T(8,128)(2,1)S(1)} %bitcast.2) | data formatting | bytes 131072 | tf_op jit(solution)/shard_map/transpose | solution.py:459
